TPU v7x, 32 devices: a whole 2x2x4 slice. The times are simulated.
32 devices in a mesh: dp: 16 (over z, x, core), tensor: 2 (over y).
Axes of the slice: x: 2, y: 2, z: 4, core: 2. Of those that a mesh axis runs over, the one named last changes fastest.
Arguments:
- hidden: bfloat16 [7168, 768], P('dp'), may hold values from -6 to 6
- encoder: bfloat16 [16, 1500, 768], P('dp'), may hold values from -6 to 6
- text_len: int32 [16], P('dp'), may hold values from 56 to 448, as said below
- audio_len: int32 [16], P('dp'), may hold values from 375 to 1500, as said below
- corpus_weight: float32 [16], P('dp'), may hold values from 0.5 to 2
- cotangent: bfloat16 [7168, 768], P('dp'), may hold values from -6 to 6
- norm_gain: float32 [3, 768], replicated, may hold values from 0.5 to 1.5
- norm_bias: float32 [3, 768], replicated, may hold values from -1.5 to 1.5
- self_proj: bfloat16 [3, 768, 768], P(None, None, 'tensor'), may hold values from -0.21875 to 0.21875
- self_bias: float32 [2, 768], P(None, 'tensor'), may hold values from -1.5 to 1.5
- cross_proj: bfloat16 [3, 768, 768], P(None, None, 'tensor'), may hold values from -0.21875 to 0.21875
- cross_bias: float32 [2, 768], P(None, 'tensor'), may hold values from -1.5 to 1.5
- out_proj: bfloat16 [2, 768, 768], P(None, 'tensor'), may hold values from -1.75 to 1.75
- out_bias: float32 [2, 768], replicated, may hold values from -1.5 to 1.5
- fc1_weight: bfloat16 [768, 3072], P(None, 'tensor'), may hold values from -0.21875 to 0.21875
- fc1_bias: float32 [3072], P('tensor'), may hold values from -1.5 to 1.5
- fc2_weight: bfloat16 [3072, 768], P('tensor'), may hold values from -0.109375 to 0.109375
- fc2_bias: float32 [768], replicated, may hold values from -1.5 to 1.5
Outputs:
- output: bfloat16 [7168, 768], P('dp')
- grad_hidden: bfloat16 [7168, 768], P('dp')
- grad_encoder: float32 [16, 1500, 768], P('dp')
- norm_gain_grad: float32 [3, 768], replicated
- norm_bias_grad: float32 [3, 768], replicated
- self_proj_grad: float32 [3, 768, 768], P(None, None, 'tensor')
- self_bias_grad: float32 [2, 768], P(None, 'tensor')
- cross_proj_grad: float32 [3, 768, 768], P(None, None, 'tensor')
- cross_bias_grad: float32 [2, 768], P(None, 'tensor')
- out_proj_grad: float32 [2, 768, 768], P(None, 'tensor')
- out_bias_grad: float32 [2, 768], replicated
- fc1_weight_grad: float32 [768, 3072], P(None, 'tensor')
- fc1_bias_grad: float32 [3072], P('tensor')
- fc2_weight_grad: float32 [3072, 768], P('tensor')
- fc2_bias_grad: float32 [768], replicated
Inputs may be any that keep to these rules, and one draw needn't show every extreme that they name: `text_len`: one sequence of the batch has all 448 tokens. `audio_len`: one sequence of the batch has all 1500 frames.
All inputs are finite; a program needn't handle non-finite values.
Results may differ from a plain program's by a relative error of at most 0.023.
The roundings to bfloat16 on the way count: a program that leaves them out, or rounds other values in their place, can miss the bound.
Values sent between devices are 32-bit elements; how exact they have to be, the bound alone decides.
No kernel may reach another device: no remote copies, remote signals or barrier semaphores. Data moves between devices by JAX's collectives and lax.ppermute only.
A program may use at most 256 MiB of HBM per device.

v0:
```python
from functools import partial

import jax
import jax.numpy as jnp
from jax import lax
from jax.sharding import PartitionSpec as P

HEAD_DIM = 64


epsilon = 1e-05
masked_value = -1e30


def norm_forward(values, gain, shift):
    centered = values - jnp.mean(values, axis=-1, keepdims=True)
    inverse = lax.rsqrt(jnp.mean(centered * centered, axis=-1, keepdims=True) + epsilon)
    unit = centered * inverse
    return (unit * gain + shift, unit, inverse)


def norm_backward(incoming, unit, inverse, gain):
    scaled = incoming * gain
    scaled_mean = jnp.mean(scaled, axis=-1, keepdims=True)
    along_unit = jnp.mean(scaled * unit, axis=-1, keepdims=True)
    input_grad = inverse * (scaled - scaled_mean - unit * along_unit)
    return (input_grad, jnp.sum(incoming * unit, axis=0), jnp.sum(incoming, axis=0))


def split_heads(values, sequences):
    return values.reshape(sequences, -1, values.shape[-1] // HEAD_DIM, HEAD_DIM)


def head_scores(queries, keys_all, allowed):
    raw = jnp.einsum("sqhc,skhc->shqk", queries, keys_all, preferred_element_type=jnp.float32)
    return jnp.where(allowed[:, None], raw, masked_value)


def attend_forward(queries, keys_all, values_all, allowed):
    masked = head_scores(queries, keys_all, allowed)
    largest = jnp.max(masked, axis=-1, keepdims=True)
    weights = jnp.exp(masked - largest)
    totals = jnp.sum(weights, axis=-1, keepdims=True)
    probs_low = (weights / totals).astype(jnp.bfloat16)
    mixed = jnp.einsum("shqk,skhc->sqhc", probs_low, values_all, preferred_element_type=jnp.float32)
    flat = mixed.reshape(mixed.shape[0] * mixed.shape[1], mixed.shape[2] * mixed.shape[3])
    return (flat.astype(jnp.bfloat16), largest + jnp.log(totals))


def attend_backward(queries, keys_all, values_all, allowed, log_total, grad_mixed):
    masked = head_scores(queries, keys_all, allowed)
    probs = jnp.exp(masked - log_total)
    grad_heads = grad_mixed.reshape(queries.shape)
    grad_values = jnp.einsum(
        "shqk,sqhc->skhc",
        probs.astype(jnp.bfloat16),
        grad_heads,
        preferred_element_type=jnp.float32,
    )
    grad_probs = jnp.einsum(
        "sqhc,skhc->shqk", grad_heads, values_all, preferred_element_type=jnp.float32
    )
    row_terms = jnp.sum(grad_probs * probs, axis=-1, keepdims=True)
    grad_scores = (probs * (grad_probs - row_terms)).astype(jnp.bfloat16)
    grad_query = jnp.einsum(
        "shqk,skhc->sqhc", grad_scores, keys_all, preferred_element_type=jnp.float32
    )
    grad_keys = jnp.einsum(
        "shqk,sqhc->skhc", grad_scores, queries, preferred_element_type=jnp.float32
    )
    width = queries.shape[2] * queries.shape[3]
    return (
        grad_query.reshape(-1, width).astype(jnp.bfloat16),
        grad_keys.reshape(-1, width).astype(jnp.bfloat16),
        grad_values.reshape(-1, width).astype(jnp.bfloat16),
    )


def flatten_padded(arrays, count):
    flat = jnp.concatenate([item.reshape(-1) for item in arrays])
    extra = -flat.shape[0] % count
    return flat


def unflatten(flat, templates):
    pieces = []
    offset = 0
    for item in templates:
        length = item.size
        pieces.append(flat[offset : offset + length].reshape(item.shape))
        offset = offset + length
    return tuple(pieces)


def layer_forward(hidden, encoder, self_allowed, cross_allowed, weights):
    (
        norm_gain,
        norm_bias,
        self_proj,
        self_bias,
        cross_proj,
        cross_bias,
        out_proj,
        out_bias,
        fc1_weight,
        fc1_bias,
        fc2_weight,
        fc2_bias,
    ) = weights
    sequences = encoder.shape[0]
    scale = HEAD_DIM ** (-0.5)
    residual = hidden.astype(jnp.float32)
    normed, unit_self, inverse_self = norm_forward(residual, norm_gain[0], norm_bias[0])
    normed_self = normed.astype(jnp.bfloat16)
    projected = jnp.einsum(
        "td,gde->gte", normed_self, self_proj, preferred_element_type=jnp.float32
    )
    query_self = ((projected[0] + self_bias[0]) * scale).astype(jnp.bfloat16)
    keys_self = projected[1].astype(jnp.bfloat16)
    values_self = (projected[2] + self_bias[1]).astype(jnp.bfloat16)
    heads_self, total_self = attend_forward(
        split_heads(query_self, sequences),
        split_heads(keys_self, sequences),
        split_heads(values_self, sequences),
        self_allowed,
    )
    partial_self = jnp.dot(heads_self, out_proj[0], preferred_element_type=jnp.float32)
    first = residual + lax.psum(partial_self, "tensor") + out_bias[0]
    normed, unit_cross, inverse_cross = norm_forward(first, norm_gain[1], norm_bias[1])
    normed_cross = normed.astype(jnp.bfloat16)
    query_cross = (
        (jnp.dot(normed_cross, cross_proj[0], preferred_element_type=jnp.float32) + cross_bias[0])
        * scale
    ).astype(jnp.bfloat16)
    encoder_flat = encoder.reshape(-1, encoder.shape[-1])
    frame_proj = jnp.einsum(
        "td,gde->gte", encoder_flat, cross_proj[1:], preferred_element_type=jnp.float32
    )
    keys_cross = frame_proj[0].astype(jnp.bfloat16)
    values_cross = (frame_proj[1] + cross_bias[1]).astype(jnp.bfloat16)
    heads_cross, total_cross = attend_forward(
        split_heads(query_cross, sequences),
        split_heads(keys_cross, sequences),
        split_heads(values_cross, sequences),
        cross_allowed,
    )
    partial_cross = jnp.dot(heads_cross, out_proj[1], preferred_element_type=jnp.float32)
    second = first + lax.psum(partial_cross, "tensor") + out_bias[1]
    normed, unit_mlp, inverse_mlp = norm_forward(second, norm_gain[2], norm_bias[2])
    normed_mlp = normed.astype(jnp.bfloat16)
    pre_act = jnp.dot(normed_mlp, fc1_weight, preferred_element_type=jnp.float32) + fc1_bias
    inner = jax.nn.gelu(pre_act, approximate=False).astype(jnp.bfloat16)
    partial_mlp = jnp.dot(inner, fc2_weight, preferred_element_type=jnp.float32)
    result = second + lax.psum(partial_mlp, "tensor") + fc2_bias
    kept = {
        "unit_self": unit_self,
        "inverse_self": inverse_self,
        "normed_self": normed_self,
        "query_self": query_self,
        "keys_self": keys_self,
        "values_self": values_self,
        "heads_self": heads_self,
        "total_self": total_self,
        "unit_cross": unit_cross,
        "inverse_cross": inverse_cross,
        "normed_cross": normed_cross,
        "query_cross": query_cross,
        "keys_cross": keys_cross,
        "values_cross": values_cross,
        "heads_cross": heads_cross,
        "total_cross": total_cross,
        "unit_mlp": unit_mlp,
        "inverse_mlp": inverse_mlp,
        "normed_mlp": normed_mlp,
        "pre_act": pre_act,
        "inner": inner,
    }
    return (result, kept)


def per_device(
    hidden,
    encoder,
    text_len,
    audio_len,
    corpus_weight,
    cotangent,
    norm_gain,
    norm_bias,
    self_proj,
    self_bias,
    cross_proj,
    cross_bias,
    out_proj,
    out_bias,
    fc1_weight,
    fc1_bias,
    fc2_weight,
    fc2_bias,
):
    weights = (
        norm_gain,
        norm_bias,
        self_proj,
        self_bias,
        cross_proj,
        cross_bias,
        out_proj,
        out_bias,
        fc1_weight,
        fc1_bias,
        fc2_weight,
        fc2_bias,
    )
    sequences, frame_count, width = encoder.shape
    length = hidden.shape[0] // sequences
    scale = HEAD_DIM ** (-0.5)
    members = lax.axis_size("dp")
    places = jnp.arange(length)
    frame_places = jnp.arange(frame_count)
    self_allowed = (places[None, :, None] >= places[None, None, :]) & (
        places[None, None, :] < text_len[:, None, None]
    )
    cross_allowed = jnp.broadcast_to(
        frame_places[None, None, :] < audio_len[:, None, None], (sequences, length, frame_count)
    )
    result, kept = layer_forward(hidden, encoder, self_allowed, cross_allowed, weights)
    again_input, again_encoder, _ = lax.optimization_barrier((hidden, encoder, result))
    kept = layer_forward(again_input, again_encoder, self_allowed, cross_allowed, weights)[1]
    live = (
        (places[None, :] < text_len[:, None]).astype(jnp.float32) * corpus_weight[:, None]
    ).reshape(-1, 1)
    grad_y = cotangent.astype(jnp.float32) * live
    grad_low = grad_y.astype(jnp.bfloat16)
    fc2_weight_grad = jnp.einsum(
        "tf,td->fd", kept["inner"], grad_low, preferred_element_type=jnp.float32
    )
    fc2_bias_grad = jnp.sum(grad_y, axis=0)
    grad_inner = jnp.einsum("td,fd->tf", grad_low, fc2_weight, preferred_element_type=jnp.float32)
    _, gelu_back = jax.vjp(partial(jax.nn.gelu, approximate=False), kept["pre_act"])
    grad_pre = gelu_back(grad_inner)[0].astype(jnp.bfloat16)
    fc1_weight_grad = jnp.einsum(
        "td,tf->df", kept["normed_mlp"], grad_pre, preferred_element_type=jnp.float32
    )
    fc1_bias_grad = jnp.sum(grad_pre.astype(jnp.float32), axis=0)
    grad_normed = lax.psum(
        jnp.einsum("tf,df->td", grad_pre, fc1_weight, preferred_element_type=jnp.float32), "tensor"
    )
    back_input, gain_mlp, shift_mlp = norm_backward(
        grad_normed, kept["unit_mlp"], kept["inverse_mlp"], norm_gain[2]
    )
    grad_second = grad_y + back_input
    second_low = grad_second.astype(jnp.bfloat16)
    out_cross_grad = jnp.einsum(
        "te,td->ed", kept["heads_cross"], second_low, preferred_element_type=jnp.float32
    )
    out_cross_bias = jnp.sum(grad_second, axis=0)
    grad_heads = jnp.einsum(
        "td,ed->te", second_low, out_proj[1], preferred_element_type=jnp.float32
    ).astype(jnp.bfloat16)
    grad_query, grad_keys, grad_values = attend_backward(
        split_heads(kept["query_cross"], sequences),
        split_heads(kept["keys_cross"], sequences),
        split_heads(kept["values_cross"], sequences),
        cross_allowed,
        kept["total_cross"],
        grad_heads,
    )
    grad_query = grad_query * scale
    query_weight_grad = jnp.einsum(
        "td,te->de", kept["normed_cross"], grad_query, preferred_element_type=jnp.float32
    )
    encoder_flat = encoder.reshape(-1, width)
    grad_frames = jnp.stack([grad_keys, grad_values])
    frame_weight_grad = jnp.einsum(
        "td,gte->gde", encoder_flat, grad_frames, preferred_element_type=jnp.float32
    )
    cross_proj_grad = jnp.concatenate([query_weight_grad[None], frame_weight_grad], axis=0)
    cross_bias_grad = jnp.stack(
        [
            jnp.sum(grad_query.astype(jnp.float32), axis=0),
            jnp.sum(grad_values.astype(jnp.float32), axis=0),
        ]
    )
    normed_term = jnp.einsum(
        "te,de->td", grad_query, cross_proj[0], preferred_element_type=jnp.float32
    )
    encoder_term = jnp.einsum(
        "gte,gde->td", grad_frames, cross_proj[1:], preferred_element_type=jnp.float32
    )
    grad_normed, grad_frame_sum = lax.psum((normed_term, encoder_term), "tensor")
    back_input, gain_cross, shift_cross = norm_backward(
        grad_normed, kept["unit_cross"], kept["inverse_cross"], norm_gain[1]
    )
    grad_first = grad_second + back_input
    first_low = grad_first.astype(jnp.bfloat16)
    out_self_grad = jnp.einsum(
        "te,td->ed", kept["heads_self"], first_low, preferred_element_type=jnp.float32
    )
    out_self_bias = jnp.sum(grad_first, axis=0)
    grad_heads = jnp.einsum(
        "td,ed->te", first_low, out_proj[0], preferred_element_type=jnp.float32
    ).astype(jnp.bfloat16)
    grad_query, grad_keys, grad_values = attend_backward(
        split_heads(kept["query_self"], sequences),
        split_heads(kept["keys_self"], sequences),
        split_heads(kept["values_self"], sequences),
        self_allowed,
        kept["total_self"],
        grad_heads,
    )
    grad_project = jnp.stack([grad_query * scale, grad_keys, grad_values])
    self_proj_grad = jnp.einsum(
        "td,gte->gde", kept["normed_self"], grad_project, preferred_element_type=jnp.float32
    )
    self_bias_grad = jnp.stack(
        [
            jnp.sum(grad_project[0].astype(jnp.float32), axis=0),
            jnp.sum(grad_values.astype(jnp.float32), axis=0),
        ]
    )
    grad_normed = lax.psum(
        jnp.einsum("gte,gde->td", grad_project, self_proj, preferred_element_type=jnp.float32),
        "tensor",
    )
    back_input, gain_self, shift_self = norm_backward(
        grad_normed, kept["unit_self"], kept["inverse_self"], norm_gain[0]
    )
    grad_hidden = (grad_first + back_input).astype(jnp.bfloat16)
    norm_gain_grad = jnp.stack([gain_self, gain_cross, gain_mlp])
    norm_bias_grad = jnp.stack([shift_self, shift_cross, shift_mlp])
    out_proj_grad = jnp.stack([out_self_grad, out_cross_grad])
    out_bias_grad = jnp.stack([out_self_bias, out_cross_bias])
    every = (
        norm_gain_grad,
        norm_bias_grad,
        self_proj_grad,
        self_bias_grad,
        cross_proj_grad,
        cross_bias_grad,
        out_proj_grad,
        out_bias_grad,
        fc1_weight_grad,
        fc1_bias_grad,
        fc2_weight_grad,
        fc2_bias_grad,
    )
    every_share = lax.psum_scatter(
        flatten_padded(every, members), "dp", scatter_dimension=0, tiled=True
    )
    every_whole = lax.all_gather(every_share, "dp", axis=0, tiled=True)
    (
        norm_gain_grad,
        norm_bias_grad,
        self_proj_grad,
        self_bias_grad,
        cross_proj_grad,
        cross_bias_grad,
        out_proj_grad,
        out_bias_grad,
        fc1_weight_grad,
        fc1_bias_grad,
        fc2_weight_grad,
        fc2_bias_grad,
    ) = unflatten(every_whole, every)
    grad_encoder = grad_frame_sum.reshape(encoder.shape)
    return (
        result.astype(jnp.bfloat16),
        grad_hidden,
        grad_encoder,
        norm_gain_grad,
        norm_bias_grad,
        self_proj_grad,
        self_bias_grad,
        cross_proj_grad,
        cross_bias_grad,
        out_proj_grad,
        out_bias_grad,
        fc1_weight_grad,
        fc1_bias_grad,
        fc2_weight_grad,
        fc2_bias_grad,
    )


def solution(mesh):
    placed = (
        P("dp", None),
        P("dp", None, None),
        P("dp"),
        P("dp"),
        P("dp"),
        P("dp", None),
        P(),
        P(),
        P(None, None, "tensor"),
        P(None, "tensor"),
        P(None, None, "tensor"),
        P(None, "tensor"),
        P(None, "tensor", None),
        P(),
        P(None, "tensor"),
        P("tensor"),
        P("tensor", None),
        P(),
    )
    return jax.shard_map(
        per_device,
        mesh=mesh,
        in_specs=placed,
        out_specs=(
            P("dp", None),
            P("dp", None),
            P("dp", None, None),
            P(),
            P(),
            P(None, None, "tensor"),
            P(None, "tensor"),
            P(None, None, "tensor"),
            P(None, "tensor"),
            P(None, "tensor", None),
            P(),
            P(None, "tensor"),
            P("tensor"),
            P("tensor", None),
            P(),
        ),
        check_vma=False,
    )
```

profile of v0, /device:TPU:0, one launch (start us, length us, event | category | flops | bytes accessed | tf_op | source)
XLA Modules:
  0.0 1546.6 jit_solution(9233833121144126764)
XLA Ops:
  45.0 36.3 %all-reduce.14.cloned.1.call-done = f32[448,768]{1,0:T(8,128)} async-done(((f32[448,768]{1,0:T(8,128)}), f32[448,768]{1,0:T(8,128)}) %all-reduce.14.cloned.1.call-update) | async-done | bytes 1376272 | tf_op jit(solution)/shard_map/psum | solution.py:128
  87.8 9.3 fusion.228
  97.2 9.0 fusion.91
  108.1 47.1 %all-reduce.16.cloned.1.call-done = f32[448,768]{1,0:T(8,128)} async-done(((f32[448,768]{1,0:T(8,128)}), f32[448,768]{1,0:T(8,128)}) %all-reduce.16.cloned.1.call-update) | async-done | bytes 1376272 | tf_op jit(solution)/shard_map/psum | solution.py:148
  158.7 11.0 fusion.94
  169.8 47.3 %all-reduce.18.cloned.1.call-done = f32[448,768]{1,0:T(8,128)} async-done(((f32[448,768]{1,0:T(8,128)}), f32[448,768]{1,0:T(8,128)}) %all-reduce.18.cloned.1.call-update) | async-done | bytes 1376272 | tf_op jit(solution)/shard_map/psum | solution.py:154
  251.6 34.8 %all-reduce.20.cloned.1.call-done = f32[448,768]{1,0:T(8,128)} async-done(((f32[448,768]{1,0:T(8,128)}), f32[448,768]{1,0:T(8,128)}) %all-reduce.20.cloned.1.call-update) | async-done | bytes 1376272 | tf_op jit(solution)/shard_map/psum | solution.py:128
  294.0 9.0 select_reduce_fusion.1
  303.0 9.2 fusion.2
  312.2 8.4 fusion.90
  324.4 45.9 %all-reduce.22.cloned.1.call-done = f32[448,768]{1,0:T(8,128)} async-done(((f32[448,768]{1,0:T(8,128)}), f32[448,768]{1,0:T(8,128)}) %all-reduce.22.cloned.1.call-update) | async-done | bytes 1376272 | tf_op jit(solution)/shard_map/psum | solution.py:148
  372.8 6.6 fusion.29
  388.1 44.9 %all-reduce.24.cloned.1.call-done = f32[448,768]{1,0:T(8,128)} async-done(((f32[448,768]{1,0:T(8,128)}), f32[448,768]{1,0:T(8,128)}) %all-reduce.24.cloned.1.call-update) | async-done | bytes 1376272 | tf_op jit(solution)/shard_map/psum | solution.py:246
  439.1 11.9 multiply_reduce_fusion
  451.0 11.7 multiply_convert_fusion
  471.6 10.4 convert_reduce_fusion.1
  483.8 5.9 convolution_bitcast_fusion.1
  489.7 27.7 %all-reduce.26.cloned.1.call-done = f32[448,768]{1,0:T(8,128)} async-done(((f32[448,768]{1,0:T(8,128)}), f32[448,768]{1,0:T(8,128)}) %all-reduce.26.cloned.1.call-update) | async-done | bytes 1376272 | tf_op jit(solution)/shard_map/psum | solution.py:291
  547.5 5.9 reshape.727
  553.4 6.5 fusion.79
  603.9 84.4 %all-reduce.32.cloned.1.call-done = (f32[448,768]{1,0:T(8,128)}, f32[1,1500,768]{2,1,0:T(8,128)}) async-done(((f32[448,768]{1,0:T(8,128)}, f32[1,1500,768]{2,1,0:T(8,128)}), (f32[448,768]{1,0:T(8,128)}, f32[1,1500,768]{2,1,0:T(8,128)})) %all-reduce.32.cloned.1.call-update) | async-done | bytes 5984272 | tf_op jit(solution)/shard_map/psum | solution.py:322
  693.1 31.1 %dynamic-update-slice.3 = f32[4728576]{0:T(1024)} dynamic-update-slice(f32[4728576]{0:T(1024)} %constant_dynamic-update-slice_fusion.7, f32[884736]{0:T(1024)} %reshape.721, s32[]{} %constant.122) | dynamic-update-slice | bytes 7077892
  725.5 31.1 %dynamic-update-slice.5 = f32[4728576]{0:T(1024)} dynamic-update-slice(f32[4728576]{0:T(1024)} %constant_dynamic-update-slice_fusion.6, f32[884736]{0:T(1024)} %reshape.723, s32[]{} %constant.124) | dynamic-update-slice | bytes 7077892
  762.5 41.0 %dynamic-update-slice.9 = f32[4728576]{0:T(1024)} dynamic-update-slice(f32[4728576]{0:T(1024)} %constant_dynamic-update-slice_fusion.3, f32[1179648]{0:T(1024)} %reshape.727, s32[]{} %constant.128) | dynamic-update-slice | bytes 9437188
  811.9 329.2 %all-reduce.30.cloned.1.call-done = f32[4728576]{0:T(1024)} async-done(((f32[4728576]{0:T(1024)}), f32[4728576]{0:T(1024)}) %all-reduce.30.cloned.1.call-update) | async-done | bytes 18914320
  1142.8 6.9 broadcast.455
  1149.7 10.9 dynamic-update-slice
  1160.6 12.6 copy.119
  1174.6 317.5 %all-reduce.28.cloned.1.call-done = f32[4728576]{0:T(1024)} async-done(((f32[4728576]{0:T(1024)}), f32[4728576]{0:T(1024)}) %all-reduce.28.cloned.1.call-update) | async-done | bytes 18914320
  1492.1 6.4 fusion.220
  1504.2 6.0 slice.243
  1510.2 6.5 fusion.222
  (425 shorter events, 245.0 us)
Async XLA Ops:
  7.2 151.5 %copy-start = (bf16[768,1536]{1,0:T(8,128)(2,1)S(1)}, bf16[768,1536]{1,0:T(8,128)(2,1)}, u32[]{:S(2)}) copy-start(bf16[768,1536]{1,0:T(8,128)(2,1)} %param.32) | copy-start | bytes 7077892
  7.2 74.1 %all-reduce.14.cloned.1.call-start = ((), (), s32[]{:S(2)}) async-start(), calls=%async_computation | async-start | bytes 2752512 | tf_op jit(solution)/shard_map/psum | solution.py:128
  11.1 147.6 %copy-start.61 = (f32[768]{0:T(1024)}, f32[768]{0:T(1024)S(1)}, u32[]{:S(2)}) copy-start(f32[768]{0:T(1024)S(1)} %get-tuple-element.144) | copy-start | bytes 9220
  11.1 147.6 %copy-start.106 = (f32[768]{0:T(1024)}, f32[768]{0:T(1024)S(1)}, u32[]{:S(2)}) copy-start(f32[768]{0:T(1024)S(1)} %get-tuple-element.79) | copy-start | bytes 9220
  11.1 209.5 %copy-start.59 = (f32[768]{0:T(1024)}, f32[768]{0:T(1024)S(1)}, u32[]{:S(2)}) copy-start(f32[768]{0:T(1024)S(1)} %get-tuple-element.143) | copy-start | bytes 9220
  11.1 209.5 %copy-start.102 = (f32[768]{0:T(1024)}, f32[768]{0:T(1024)S(1)}, u32[]{:S(2)}) copy-start(f32[768]{0:T(1024)S(1)} %get-tuple-element.80) | copy-start | bytes 9220
  11.1 277.2 %copy-start.65 = (f32[768]{0:T(1024)}, f32[768]{0:T(1024)S(1)}, u32[]{:S(2)}) copy-start(f32[768]{0:T(1024)S(1)} %get-tuple-element.142) | copy-start | bytes 9220
  11.1 277.2 %copy-start.104 = (f32[768]{0:T(1024)}, f32[768]{0:T(1024)S(1)}, u32[]{:S(2)}) copy-start(f32[768]{0:T(1024)S(1)} %get-tuple-element.81) | copy-start | bytes 9220
  19.0 214.7 %copy-start.24 = (pred[448,448]{0,1:T(8,128)(4,1)}, pred[448,448]{0,1:T(8,128)(4,1)S(1)}, u32[]{:S(2)}) copy-start(pred[448,448]{0,1:T(8,128)(4,1)S(1)} %fusion.100) | copy-start | bytes 602116
  19.1 211.1 %copy-start.57 = (f32[6,64]{1,0:T(8,128)}, f32[6,64]{1,0:T(8,128)S(1)}, u32[]{:S(2)}) copy-start(f32[6,64]{1,0:T(8,128)S(1)} %add.296) | copy-start | bytes 4612
  20.4 213.3 %copy-start.89 = (f32[6,64]{1,0:T(8,128)}, f32[6,64]{1,0:T(8,128)S(1)}, u32[]{:S(2)}) copy-start(f32[6,64]{1,0:T(8,128)S(1)} %add.293) | copy-start | bytes 4612
  31.3 123.9 %all-reduce.16.cloned.1.call-start = ((), (), s32[]{:S(2)}) async-start(), calls=%async_computation.1 | async-start | bytes 2752512 | tf_op jit(solution)/shard_map/psum | solution.py:148
  41.8 55.3 %copy-start.92 = (f32[6,64]{1,0:T(8,128)}, f32[6,64]{1,0:T(8,128)S(1)}, u32[]{:S(2)}) copy-start(f32[6,64]{1,0:T(8,128)S(1)} %add.303) | copy-start | bytes 4612
  45.0 42.9 %copy-start.54 = (pred[1500]{0:T(1024)(128)(4,1)}, pred[1500]{0:T(1024)(128)(4,1)S(1)}, u32[]{:S(2)}) copy-start(pred[1500]{0:T(1024)(128)(4,1)S(1)} %iota_compare_fusion.1) | copy-start | bytes 4504
  45.0 110.2 %copy-start.67 = (f32[768]{0:T(1024)}, f32[768]{0:T(1024)S(1)}, u32[]{:S(2)}) copy-start(f32[768]{0:T(1024)S(1)} %get-tuple-element.82) | copy-start | bytes 9220
  107.8 109.3 %all-reduce.18.cloned.1.call-start = ((), (), s32[]{:S(2)}) async-start(), calls=%async_computation.2 | async-start | bytes 2752512 | tf_op jit(solution)/shard_map/psum | solution.py:154
  158.7 58.4 %copy-start.99 = (f32[768]{0:T(1024)S(1)}, f32[768]{0:T(1024)}, u32[]{:S(2)}) copy-start(f32[768]{0:T(1024)} %param.35) | copy-start | bytes 9220
  169.8 116.6 %all-reduce.20.cloned.1.call-start = ((), (), s32[]{:S(2)}) async-start(), calls=%async_computation.3 | async-start | bytes 2752512 | tf_op jit(solution)/shard_map/psum | solution.py:128
  239.0 131.3 %all-reduce.22.cloned.1.call-start = ((), (), s32[]{:S(2)}) async-start(), calls=%async_computation.4 | async-start | bytes 2752512 | tf_op jit(solution)/shard_map/psum | solution.py:148
  323.0 110.0 %all-reduce.24.cloned.1.call-start = ((), (), s32[]{:S(2)}) async-start(), calls=%async_computation.5 | async-start | bytes 2752512 | tf_op jit(solution)/shard_map/psum | solution.py:246
  385.5 47.4 %copy-start.12 = (f32[448,768]{1,0:T(8,128)S(1)}, f32[448,768]{1,0:T(8,128)}, u32[]{:S(2)}) copy-start(f32[448,768]{1,0:T(8,128)} %copy-done.11) | copy-start | bytes 4128772
  385.5 50.1 %copy-start.35 = (bf16[448,768]{1,0:T(8,128)(2,1)S(1)}, bf16[448,768]{1,0:T(8,128)(2,1)}, u32[]{:S(2)}) copy-start(bf16[448,768]{1,0:T(8,128)(2,1)} %param.23) | copy-start | bytes 2064388
  385.5 50.1 %copy-start.63 = (f32[768]{0:T(1024)S(1)}, f32[768]{0:T(1024)}, u32[]{:S(2)}) copy-start(f32[768]{0:T(1024)} %copy-done.61) | copy-start | bytes 9220
  385.6 50.1 %copy-start.69 = (f32[448]{0:T(512)S(1)}, f32[448]{0:T(512)}, u32[]{:S(2)}) copy-start(f32[448]{0:T(512)} %copy-done.68) | copy-start | bytes 5380
  385.6 50.1 %copy-start.76 = (f32[448]{0:T(512)S(1)}, f32[448]{0:T(512)}, u32[]{:S(2)}) copy-start(f32[448]{0:T(512)} %broadcast_select_fusion) | copy-start | bytes 5380
  385.6 50.1 %copy-start.79 = (f32[448]{0:T(512)S(1)}, f32[448]{0:T(512)}, u32[]{:S(2)}) copy-start(f32[448]{0:T(512)} %copy-done.78) | copy-start | bytes 5380
  385.6 131.9 %all-reduce.26.cloned.1.call-start = ((), (), s32[]{:S(2)}) async-start(), calls=%async_computation.6 | async-start | bytes 2752512 | tf_op jit(solution)/shard_map/psum | solution.py:291
  388.1 62.9 %copy-start.52 = (f32[6,448]{1,0:T(8,128)}, f32[6,448]{1,0:T(8,128)S(1)}, u32[]{:S(2)}) copy-start(f32[6,448]{1,0:T(8,128)S(1)} %log_add_fusion.1) | copy-start | bytes 32260
  470.1 218.2 %all-reduce.32.cloned.1.call-start = ((), (), s32[]{:S(2)}) async-start(), calls=%async_computation.9 | async-start | bytes 11993088 | tf_op jit(solution)/shard_map/psum | solution.py:322
  541.0 600.1 %all-reduce.30.cloned.1.call-start = ((), (), s32[]{:S(2)}) async-start(), calls=%async_computation.8 | async-start | bytes 37830656
  762.5 41.0 %copy-start.97 = (f32[1536]{0:T(1024)S(1)}, f32[1536]{0:T(1024)}, u32[]{:S(2)}) copy-start(f32[1536]{0:T(1024)} %get-tuple-element.140) | copy-start | bytes 18436
  809.4 682.7 %all-reduce.28.cloned.1.call-start = ((), (), s32[]{:S(2)}) async-start(), calls=%async_computation.7 | async-start | bytes 37830656
  (97 other events, 517.3 us)
Sparse Core Ops, SparseCore 0:
  31.4 49.8 all-reduce.13
  107.9 47.1 all-reduce.15
  169.9 47.1 all-reduce.17
  239.1 47.1 all-reduce.19
  323.1 47.1 all-reduce.21
  385.7 47.1 all-reduce.23
  470.3 47.1 all-reduce.25
  541.1 147.1 all-reduce.31
  809.5 331.5 all-reduce.29
  1160.8 331.2 all-reduce.27
where the time goes:
time: 1560 us; the launch traced here: 1550 us
  waiting for transfers between devices  1020 us (65%)
  local copies, waits for them, and re-layouts  283 us (18%)
  matrix products  169 us (11%)
  other arithmetic  57.9 us (4%)
  between operations  19.1 us (1%)
    unnamed x12, waiting for transfers between devices  647 us
    unnamed x254, local copies, waits for them, and re-layouts  161 us
    psum x2, waiting for transfers between devices, layer_forward(): second = first + lax.psum(partial_cross, 'tensor') + out_bias[1]  93 us
    psum x1, waiting for transfers between devices, per_device(): lax.psum(jnp.einsum('gte,gde->td', grad_project, self_proj, preferred_ele...  84.4 us
    psum x2, waiting for transfers between devices, layer_forward(): first = residual + lax.psum(partial_self, 'tensor') + out_bias[0]  71.1 us
    psum x1, waiting for transfers between devices, layer_forward(): result = second + lax.psum(partial_mlp, 'tensor') + fc2_bias  47.3 us
    psum x1, waiting for transfers between devices, per_device(): lax.psum(jnp.einsum('tf,df->td', grad_pre, fc1_weight, preferred_element_...  44.9 us
  transfers between devices with their start and end apart: 10, of which 10 were waited for; matrix products, arithmetic and copies ran while one was open for 8% of the time, Pallas kernels for 0%

commit v1 on v0

v1 whole, which is shorter than its diff:
```python
from functools import partial

import jax
import jax.numpy as jnp
import numpy as np
from jax import lax
from jax.experimental import pallas as pl
from jax.experimental.pallas import tpu as pltpu
from jax.sharding import PartitionSpec as P

HEAD_DIM = 64
SCALE = HEAD_DIM ** (-0.5)
PAIR = 2 * HEAD_DIM
LANES = 128
epsilon = 1e-05
masked_value = -1e30
f32 = jnp.float32
bf16 = jnp.bfloat16


def dot(a, b, ca, cb):
    return lax.dot_general(a, b, (((ca,), (cb,)), ((), ())), preferred_element_type=f32)


def norm_forward(values, gain, shift):
    centered = values - jnp.mean(values, axis=-1, keepdims=True)
    inverse = lax.rsqrt(jnp.mean(centered * centered, axis=-1, keepdims=True) + epsilon)
    unit = centered * inverse
    return (unit * gain + shift, unit, inverse)


def norm_backward(incoming, unit, inverse, gain):
    scaled = incoming * gain
    scaled_mean = jnp.mean(scaled, axis=-1, keepdims=True)
    along_unit = jnp.mean(scaled * unit, axis=-1, keepdims=True)
    return inverse * (scaled - scaled_mean - unit * along_unit)


def lane_masks(rows):
    lanes = lax.broadcasted_iota(jnp.int32, (rows, PAIR), 1)
    return lanes < HEAD_DIM


def allowed_of(length, rows, columns, causal):
    places = lax.broadcasted_iota(jnp.int32, (rows, columns), 1)
    allowed = places < length
    if causal:
        allowed = allowed & (places <= lax.broadcasted_iota(jnp.int32, (rows, columns), 0))
    return allowed


def attend_forward_kernel(causal, length_ref, q_ref, k_ref, v_ref, heads_ref, weights_ref, inverse_ref):
    rows, columns = q_ref.shape[0], k_ref.shape[0]
    length = length_ref[0]
    first_lanes = lane_masks(rows)
    if causal:
        allowed = allowed_of(length, rows, columns, True)
    else:
        places = lax.broadcasted_iota(jnp.int32, (1, columns), 1)
        shift = jnp.where(places < length, 0.0, masked_value)
    q = q_ref[...]
    k = k_ref[...]
    v = v_ref[...]
    mixed = []
    inverses = []
    for head in range(2):
        mine = first_lanes if head == 0 else jnp.logical_not(first_lanes)
        scores = dot(jnp.where(mine, q, jnp.zeros_like(q)), k, 1, 1)
        if causal:
            scores = jnp.where(allowed, scores, masked_value)
        else:
            scores = scores + shift
        largest = jnp.max(scores, axis=-1, keepdims=True)
        weights = jnp.exp(scores - largest)
        inverse = 1.0 / jnp.sum(weights, axis=-1, keepdims=True)
        weights = weights.astype(bf16)
        weights_ref[head] = weights
        mixed.append(dot(weights, v, 1, 0) * inverse)
        inverses.append(inverse)
    heads_ref[...] = jnp.where(first_lanes, mixed[0], mixed[1]).astype(bf16)
    inverse_ref[...] = jnp.where(first_lanes, inverses[0], inverses[1])


def attend_forward(length, q, k, v, causal):
    rows, width = q.shape
    columns = k.shape[0]
    pairs = width // PAIR
    return pl.pallas_call(
        partial(attend_forward_kernel, causal),
        grid=(pairs,),
        in_specs=[
            pl.BlockSpec(memory_space=pltpu.SMEM),
            pl.BlockSpec((rows, PAIR), lambda p: (0, p)),
            pl.BlockSpec((columns, PAIR), lambda p: (0, p)),
            pl.BlockSpec((columns, PAIR), lambda p: (0, p)),
        ],
        out_specs=[
            pl.BlockSpec((rows, PAIR), lambda p: (0, p)),
            pl.BlockSpec((2, rows, columns), lambda p: (p, 0, 0)),
            pl.BlockSpec((rows, PAIR), lambda p: (0, p)),
        ],
        out_shape=[
            jax.ShapeDtypeStruct((rows, width), bf16),
            jax.ShapeDtypeStruct((2 * pairs, rows, columns), bf16),
            jax.ShapeDtypeStruct((rows, width), f32),
        ],
        compiler_params=pltpu.CompilerParams(vmem_limit_bytes=40 * 1024 * 1024),
        cost_estimate=pl.CostEstimate(
            flops=4 * rows * columns * width * 3,
            bytes_accessed=4 * pairs * rows * columns,
            transcendentals=2 * pairs * rows * columns,
        ),
        name="attend_fwd_causal" if causal else "attend_fwd_cross",
    )(length, q, k, v)


def attend_backward_kernel(q_ref, k_ref, v_ref, weights_ref, inverse_ref, heads_ref, grad_ref, dq_ref, dk_ref, dv_ref):
    rows = q_ref.shape[0]
    first_lanes = lane_masks(rows)
    q = q_ref[...]
    k = k_ref[...]
    v = v_ref[...]
    grad = (grad_ref[...].astype(f32) * inverse_ref[...]).astype(bf16)
    along = grad.astype(f32) * heads_ref[...].astype(f32)
    dq = []
    dk = None
    dv = None
    for head in range(2):
        mine = first_lanes if head == 0 else jnp.logical_not(first_lanes)
        grad_one = jnp.where(mine, grad, jnp.zeros_like(grad))
        q_one = jnp.where(mine, q, jnp.zeros_like(q))
        row_terms = jnp.sum(jnp.where(mine, along, 0.0), axis=-1, keepdims=True)
        weights = weights_ref[head]
        grad_probs = dot(grad_one, v, 1, 1)
        grad_scores = (weights.astype(f32) * (grad_probs - row_terms)).astype(bf16)
        dv_one = dot(grad_one, weights, 0, 0)
        dk_one = dot(q_one, grad_scores, 0, 0)
        dq.append(dot(grad_scores, k, 1, 0))
        dk = dk_one if dk is None else dk + dk_one
        dv = dv_one if dv is None else dv + dv_one
    dq_ref[...] = (jnp.where(first_lanes, dq[0], dq[1]) * SCALE).astype(bf16)
    dk_ref[...] = dk.astype(bf16)
    dv_ref[...] = dv.astype(bf16)


def attend_backward(q, k, v, weights, inverse, heads, grad):
    rows, width = q.shape
    columns = k.shape[0]
    pairs = width // PAIR
    row_block = pl.BlockSpec((rows, PAIR), lambda p: (0, p))
    column_block = pl.BlockSpec((columns, PAIR), lambda p: (0, p))
    flipped = pl.BlockSpec((PAIR, columns), lambda p: (p, 0))
    return pl.pallas_call(
        attend_backward_kernel,
        grid=(pairs,),
        in_specs=[
            row_block,
            column_block,
            column_block,
            pl.BlockSpec((2, rows, columns), lambda p: (p, 0, 0)),
            row_block,
            row_block,
            row_block,
        ],
        out_specs=[row_block, flipped, flipped],
        out_shape=[
            jax.ShapeDtypeStruct((rows, width), bf16),
            jax.ShapeDtypeStruct((width, columns), bf16),
            jax.ShapeDtypeStruct((width, columns), bf16),
        ],
        compiler_params=pltpu.CompilerParams(vmem_limit_bytes=40 * 1024 * 1024),
        cost_estimate=pl.CostEstimate(
            flops=8 * rows * columns * width * 3,
            bytes_accessed=4 * pairs * rows * columns,
            transcendentals=0,
        ),
        name="attend_bwd",
    )(q, k, v, weights, inverse, heads, grad)


def join_kernel(axis, side_ref, own_ref, other_ref, whole_ref):
    own = own_ref[0].astype(f32)
    other = other_ref[0]
    first = side_ref[0] == 0
    low = jnp.where(first, own, other).astype(bf16)
    high = jnp.where(first, other, own).astype(bf16)
    extent = own.shape[axis - 1]
    if axis == 2:
        whole_ref[0, :, :extent] = low
        whole_ref[0, :, extent:] = high
    else:
        whole_ref[0, :extent, :] = low
        whole_ref[0, extent:, :] = high


def join_halves(side, own, other, axis):
    count, rows, columns = own.shape
    shape = (rows, 2 * columns) if axis == 2 else (2 * rows, columns)
    return pl.pallas_call(
        partial(join_kernel, axis),
        grid=(count,),
        in_specs=[
            pl.BlockSpec(memory_space=pltpu.SMEM),
            pl.BlockSpec((1, rows, columns), lambda p: (p, 0, 0)),
            pl.BlockSpec((1, rows, columns), lambda p: (p, 0, 0)),
        ],
        out_specs=pl.BlockSpec((1,) + shape, lambda p: (p, 0, 0)),
        out_shape=jax.ShapeDtypeStruct((count,) + shape, bf16),
        name="join_halves",
    )(side, own, other)


def swap(value):
    return lax.ppermute(value, "tensor", [(0, 1), (1, 0)])


def sum_tensor(value):
    if lax.axis_size("tensor") == 2:
        return value + swap(value)
    return lax.psum(value, "tensor")


def scatter_sum(arrays):
    members = lax.axis_size("dp")
    bits = members.bit_length() - 1
    me = lax.axis_index("dp")
    parts = [a.reshape((2,) * bits + (a.shape[0] // members, a.shape[1])) for a in arrays]
    total = None
    for bit in range(bits):
        axis = bits - 1 - bit
        side = (me >> bit) & 1
        pairs = [(i, i ^ (1 << bit)) for i in range(members)]
        mine = [lax.dynamic_index_in_dim(a, side, axis, keepdims=True) for a in parts]
        theirs = [lax.dynamic_index_in_dim(a, 1 - side, axis, keepdims=True) for a in parts]
        if len(parts) > 1:
            mine = [jnp.concatenate(mine, axis=-2)]
            theirs = [jnp.concatenate(theirs, axis=-2)]
        total = mine[0] + lax.ppermute(theirs[0], "dp", pairs)
        parts = [total]
    return total.reshape(total.shape[-2:])


def gather_parts(share, counts):
    whole = lax.all_gather(share, "dp", axis=0, tiled=False)
    pieces = []
    offset = 0
    for count in counts:
        pieces.append(whole[:, offset : offset + count].reshape(-1, share.shape[1]))
        offset += count
    return pieces


def column_blocks(value, width):
    blocks = value.shape[1] // width
    if blocks == 1:
        return value
    return jnp.concatenate([value[:, i * width : (i + 1) * width] for i in range(blocks)], axis=0)


def from_column_blocks(value, blocks):
    if blocks == 1:
        return value
    rows = value.shape[0] // blocks
    return jnp.concatenate([value[i * rows : (i + 1) * rows] for i in range(blocks)], axis=1)


def per_device(
    hidden,
    encoder,
    text_len,
    audio_len,
    corpus_weight,
    cotangent,
    norm_gain,
    norm_bias,
    self_proj,
    self_bias,
    cross_proj,
    cross_bias,
    out_proj,
    out_bias,
    fc1_weight,
    fc1_bias,
    fc2_weight,
    fc2_bias,
):
    sequences, frames, width = encoder.shape
    length = hidden.shape[0]
    members = lax.axis_size("dp")
    me = lax.axis_index("dp")
    side = lax.axis_index("tensor")
    half = self_proj.shape[2]
    padded = -(-frames // 256) * 256

    proj_rows = cross_proj.reshape(-1, half)
    out_rows = out_proj[1]
    proj_count = proj_rows.shape[0] // members
    out_count = out_rows.shape[0] // members
    out_part = lax.dynamic_slice_in_dim(out_rows, me * out_count, out_count, 0)
    part = jnp.concatenate(
        [
            lax.dynamic_slice_in_dim(proj_rows, me * proj_count, proj_count, 0).astype(f32),
            column_blocks(out_part, half).astype(f32),
            cross_bias,
        ],
        axis=0,
    )
    part = swap(part)
    sent = proj_count + 2 * out_count
    other_bias = part[sent:]
    gathered = lax.all_gather(part[:sent], "dp", axis=0, tiled=False)

    residual = hidden.astype(f32)
    normed, unit_self, inverse_self = norm_forward(residual, norm_gain[0], norm_bias[0])
    normed_self = normed.astype(bf16)
    query_self = ((dot(normed_self, self_proj[0], 1, 0) + self_bias[0]) * SCALE).astype(bf16)
    keys_self = dot(normed_self, self_proj[1], 1, 0).astype(bf16)
    values_self = (dot(normed_self, self_proj[2], 1, 0) + self_bias[1]).astype(bf16)
    heads_self, weights_self, totals_self = attend_forward(text_len, query_self, keys_self, values_self, True)
    partial_self = dot(heads_self, out_proj[0], 1, 0)
    first = residual + sum_tensor(partial_self) + out_bias[0]

    other_out = from_column_blocks(
        gathered[:, proj_count:].reshape(members, 2, out_count, half).swapaxes(0, 1).reshape(-1, half), 2
    )
    here = side.astype(jnp.int32).reshape(1)
    full_proj = join_halves(here, cross_proj, gathered[:, :proj_count].reshape(cross_proj.shape), 2)
    full_out = join_halves(here, out_proj[1:], other_out[None], 1)[0]
    full_bias = jnp.where(
        side == 0,
        jnp.concatenate([cross_bias, other_bias], axis=1),
        jnp.concatenate([other_bias, cross_bias], axis=1),
    )
    frames_in = jnp.pad(encoder.reshape(frames, width), ((0, padded - frames), (0, 0)))
    keys_cross = dot(frames_in, full_proj[1], 1, 0).astype(bf16)
    values_cross = (dot(frames_in, full_proj[2], 1, 0) + full_bias[1]).astype(bf16)

    normed, unit_cross, inverse_cross = norm_forward(first, norm_gain[1], norm_bias[1])
    normed_cross = normed.astype(bf16)
    query_cross = ((dot(normed_cross, full_proj[0], 1, 0) + full_bias[0]) * SCALE).astype(bf16)
    heads_cross, weights_cross, totals_cross = attend_forward(
        audio_len, query_cross, keys_cross, values_cross, False
    )
    second = first + dot(heads_cross, full_out, 1, 0) + out_bias[1]

    normed, unit_mlp, inverse_mlp = norm_forward(second, norm_gain[2], norm_bias[2])
    normed_mlp = normed.astype(bf16)
    pre_act = dot(normed_mlp, fc1_weight, 1, 0) + fc1_bias
    inner = jax.nn.gelu(pre_act, approximate=False).astype(bf16)
    partial_mlp = dot(inner, fc2_weight, 1, 0)

    live = jnp.where(jnp.arange(length) < text_len[0], corpus_weight[0], 0.0).reshape(-1, 1)
    grad_y = cotangent.astype(f32) * live
    grad_low = grad_y.astype(bf16)
    grad_inner = dot(grad_low, fc2_weight, 1, 1)
    _, gelu_back = jax.vjp(partial(jax.nn.gelu, approximate=False), pre_act)
    grad_pre = gelu_back(grad_inner)[0].astype(bf16)
    grad_normed = sum_tensor(dot(grad_pre, fc1_weight, 1, 1))
    fc2_weight_grad = dot(inner, grad_low, 0, 0)
    fc1_weight_grad = dot(normed_mlp, grad_pre, 0, 0)
    fc1_bias_grad = jnp.sum(grad_pre.astype(f32), axis=0)
    fc2_bias_grad = jnp.sum(grad_y, axis=0)
    fc1_blocks = fc1_weight_grad.shape[1] // width
    mlp_share = scatter_sum([fc2_weight_grad, column_blocks(fc1_weight_grad, width)])
    fc2_count = fc2_weight_grad.shape[0] // members
    fc2_weight_grad, fc1_rows = gather_parts(mlp_share, [fc2_count, mlp_share.shape[0] - fc2_count])
    fc1_weight_grad = from_column_blocks(fc1_rows, fc1_blocks)

    gain_mlp = jnp.sum(grad_normed * unit_mlp, axis=0)
    shift_mlp = jnp.sum(grad_normed, axis=0)
    grad_second = grad_y + norm_backward(grad_normed, unit_mlp, inverse_mlp, norm_gain[2])
    result = second + sum_tensor(partial_mlp) + fc2_bias

    second_low = grad_second.astype(bf16)
    grad_heads = dot(second_low, full_out, 1, 1).astype(bf16)
    grad_query, grad_keys, grad_values = attend_backward(
        query_cross, keys_cross, values_cross, weights_cross, totals_cross, heads_cross, grad_heads
    )
    grad_normed = dot(grad_query, full_proj[0], 1, 1)
    gain_cross = jnp.sum(grad_normed * unit_cross, axis=0)
    shift_cross = jnp.sum(grad_normed, axis=0)
    grad_first = grad_second + norm_backward(grad_normed, unit_cross, inverse_cross, norm_gain[1])

    own_heads = lax.dynamic_slice_in_dim(heads_cross, side * half, half, 1)
    own_query = lax.dynamic_slice_in_dim(grad_query, side * half, half, 1)
    own_keys = lax.dynamic_slice_in_dim(grad_keys, side * half, half, 0)
    own_values = lax.dynamic_slice_in_dim(grad_values, side * half, half, 0)
    out_cross_grad = dot(own_heads, second_low, 0, 0)
    cross_proj_grad = jnp.concatenate(
        [
            dot(normed_cross, own_query, 0, 0),
            dot(frames_in, own_keys, 0, 1),
            dot(frames_in, own_values, 0, 1),
        ],
        axis=0,
    )
    cross_bias_grad = jnp.stack(
        [jnp.sum(own_query.astype(f32), axis=0), jnp.sum(own_values.astype(f32), axis=1)]
    )
    out_cross_bias = jnp.sum(grad_second, axis=0)
    cross_share = scatter_sum([cross_proj_grad, column_blocks(out_cross_grad, half)])
    proj_grad_count = cross_proj_grad.shape[0] // members
    cross_rows, out_cross_rows = gather_parts(cross_share, [proj_grad_count, cross_share.shape[0] - proj_grad_count])
    grad_encoder = (
        dot(grad_keys, full_proj[1], 0, 1) + dot(grad_values, full_proj[2], 0, 1)
    )[:frames].reshape(encoder.shape)

    first_low = grad_first.astype(bf16)
    grad_heads = dot(first_low, out_proj[0], 1, 1).astype(bf16)
    grad_query, grad_keys, grad_values = attend_backward(
        query_self, keys_self, values_self, weights_self, totals_self, heads_self, grad_heads
    )
    normed_part = (
        dot(grad_query, self_proj[0], 1, 1)
        + dot(grad_keys, self_proj[1], 0, 1)
        + dot(grad_values, self_proj[2], 0, 1)
    )
    norm_part = swap(
        jnp.stack([jnp.sum(normed_part * unit_self, axis=0), jnp.sum(normed_part, axis=0)])
    ) + jnp.stack([jnp.sum(normed_part * unit_self, axis=0), jnp.sum(normed_part, axis=0)])
    gain_self, shift_self = norm_part[0], norm_part[1]
    self_proj_grad = jnp.concatenate(
        [
            dot(normed_self, grad_query, 0, 0),
            dot(normed_self, grad_keys, 0, 1),
            dot(normed_self, grad_values, 0, 1),
        ],
        axis=0,
    )
    self_bias_grad = jnp.stack(
        [jnp.sum(grad_query.astype(f32), axis=0), jnp.sum(grad_values.astype(f32), axis=1)]
    )
    out_self_grad = dot(heads_self, first_low, 0, 0)
    out_self_bias = jnp.sum(grad_first, axis=0)

    small = (
        jnp.stack([gain_self, gain_cross, gain_mlp]),
        jnp.stack([shift_self, shift_cross, shift_mlp]),
        self_bias_grad,
        cross_bias_grad,
        jnp.stack([out_self_bias, out_cross_bias]),
        fc1_bias_grad,
        fc2_bias_grad,
    )
    flat = jnp.concatenate([item.reshape(-1) for item in small])
    unit_rows = 8 * members
    small_rows = -(-flat.shape[0] // (half * unit_rows)) * unit_rows
    flat = jnp.pad(flat, (0, small_rows * half - flat.shape[0])).reshape(small_rows, half)
    self_share = scatter_sum([self_proj_grad, column_blocks(out_self_grad, half), flat])
    out_grad_count = out_self_grad.shape[0] * 2 // members
    self_rows, out_self_rows, flat = gather_parts(
        self_share, [proj_grad_count, out_grad_count, small_rows // members]
    )
    grad_normed = sum_tensor(normed_part)
    grad_hidden = (grad_first + norm_backward(grad_normed, unit_self, inverse_self, norm_gain[0])).astype(bf16)

    flat = flat.reshape(-1)
    small_out = []
    offset = 0
    for item in small:
        small_out.append(flat[offset : offset + item.size].reshape(item.shape))
        offset += item.size
    return (
        result.astype(bf16),
        grad_hidden,
        grad_encoder,
        small_out[0],
        small_out[1],
        self_rows.reshape(self_proj.shape),
        small_out[2],
        cross_rows.reshape(cross_proj.shape),
        small_out[3],
        jnp.stack([from_column_blocks(out_self_rows, 2), from_column_blocks(out_cross_rows, 2)]),
        small_out[4],
        fc1_weight_grad,
        small_out[5],
        fc2_weight_grad,
        small_out[6],
    )


def solution(mesh):
    placed = (
        P("dp", None),
        P("dp", None, None),
        P("dp"),
        P("dp"),
        P("dp"),
        P("dp", None),
        P(),
        P(),
        P(None, None, "tensor"),
        P(None, "tensor"),
        P(None, None, "tensor"),
        P(None, "tensor"),
        P(None, "tensor", None),
        P(),
        P(None, "tensor"),
        P("tensor"),
        P("tensor", None),
        P(),
    )
    return jax.shard_map(
        per_device,
        mesh=mesh,
        in_specs=placed,
        out_specs=(
            P("dp", None),
            P("dp", None),
            P("dp", None, None),
            P(),
            P(),
            P(None, None, "tensor"),
            P(None, "tensor"),
            P(None, None, "tensor"),
            P(None, "tensor"),
            P(None, "tensor", None),
            P(),
            P(None, "tensor"),
            P("tensor"),
            P("tensor", None),
            P(),
        ),
        check_vma=False,
    )
```

time: 1560 us -> 630 us (0.40)
  waiting for transfers between devices: 1020 us -> 366 us
  local copies, waits for them, and re-layouts: 283 us -> 78.6 us
  matrix products: 169 us -> 54.3 us
  Pallas kernels: 0 us -> 55.4 us
  other arithmetic: 57.9 us -> 38.5 us
    unnamed x12 -> x4, waiting for transfers between devices: 647 us -> 0.07 us
    psum x8 -> x0, waiting for transfers between devices: 368 us -> none  [the longest x2 93 us: layer_forward(): second = first + lax.psum(partial_cross, 'tensor') + out_bias[1]]
    ppermute x0 -> x18, waiting for transfers between devices: none -> 330 us  [the longest x12 236 us: scatter_sum(): total = mine[0] + lax.ppermute(theirs[0], 'dp', pairs)]
    unnamed x254 -> x133, local copies, waits for them, and re-layouts: 161 us -> 37.6 us
    dot_general x40 -> x30, matrix products: 154 us -> 54.3 us  [dot(): lax.dot_general(a, b, (((ca,), (cb,)), ((), ())), preferred_element_type=...]
    pallas_call x0 -> x6, Pallas kernels: none -> 55.4 us  [the longest x2 24.1 us: attend_forward(): pl.pallas_call(partial(attend_forward_kernel, causal), grid=(pairs,), in_...]
    reshape x14 -> x5, local copies, waits for them, and re-layouts: 42.9 us -> 0.05 us  [per_device(): flat = jnp.concatenate([item.reshape(-1) for item in small])]
    all_gather x0 -> x4, waiting for transfers between devices: none -> 36.2 us  [the longest x3 26.9 us: gather_parts(): whole = lax.all_gather(share, 'dp', axis=0, tiled=False)]
  transfers between devices with their start and end apart: 10 -> 22, of which waited for: 10 -> 17; matrix products, arithmetic and copies ran while one was open for 8% -> 16% of each run, Pallas kernels for 0% -> 1%
where the time goes in v1:
time: 630 us; the launch traced here: 627 us
  waiting for transfers between devices  366 us (58%)
  local copies, waits for them, and re-layouts  78.6 us (12%)
  Pallas kernels  55.4 us (9%)
  matrix products  54.3 us (9%)
  other arithmetic  38.5 us (6%)
  between operations  17.6 us (3%)
  starting transfers between devices  16.3 us (3%)
    ppermute x12, waiting for transfers between devices, scatter_sum(): total = mine[0] + lax.ppermute(theirs[0], 'dp', pairs)  236 us
    ppermute x6, waiting for transfers between devices, swap(): return lax.ppermute(value, 'tensor', [(0, 1), (1, 0)])  94.2 us
    dot_general x30, matrix products, dot(): lax.dot_general(a, b, (((ca,), (cb,)), ((), ())), preferred_element_type=...  54.3 us
    unnamed x133, local copies, waits for them, and re-layouts  37.6 us
    all_gather x3, waiting for transfers between devices, gather_parts(): whole = lax.all_gather(share, 'dp', axis=0, tiled=False)  26.9 us
    pallas_call x2, Pallas kernels, attend_forward(): pl.pallas_call(partial(attend_forward_kernel, causal), grid=(pairs,), in_...  24.1 us
    pallas_call x2, Pallas kernels, attend_backward(): pl.pallas_call(attend_backward_kernel, grid=(pairs,), in_specs=[row_block...  23.3 us
  transfers between devices with their start and end apart: 22, of which 17 were waited for; matrix products, arithmetic and copies ran while one was open for 16% of the time, Pallas kernels for 1%

profile of v1, /device:TPU:0, one launch (start us, length us, event | category | flops | bytes accessed | tf_op | source)
XLA Modules:
  0.0 626.8 jit_solution(7866790273145922512)
XLA Ops:
  14.2 7.3 %collective-permute-done.1 = f32[194,384]{1,0:T(8,128)S(1)} collective-permute-done((f32[194,384]{1,0:T(8,128)S(1)}, f32[194,384]{1,0:T(8,128)S(1)}, u32[]{:S(2)}, u32[]{:S(2)}) %collective-permute-start.1) | collective-permute-done | bytes 298016 | tf_op jit(solution)/shard_map/ppermute | solution.py:214
  26.4 3.5 attend_fwd_causal.1
  36.3 28.5 %collective-permute-done = f32[448,768]{1,0:T(8,128)} collective-permute-done((f32[448,768]{1,0:T(8,128)}, f32[448,768]{1,0:T(8,128)}, u32[]{:S(2)}, u32[]{:S(2)}) %collective-permute-start) | collective-permute-done | bytes 1376288 | tf_op jit(solution)/shard_map/ppermute | solution.py:214
  68.4 9.3 %all-gather.9.cloned.1.call-done = f32[3072,384]{1,0:T(8,128)} async-done(((f32[192,384]{1,0:T(8,128)}), f32[3072,384]{1,0:T(8,128)}) %all-gather.9.cloned.1.call-update) | async-done | bytes 4718608 | tf_op jit(solution)/shard_map/all_gather | solution.py:311
  77.8 4.0 slice.282
  84.1 5.3 join_halves.2
  89.4 5.5 convolution_convert_fusion.k_ref
  95.0 4.8 add_convert_fusion.v_ref
  106.8 20.6 %attend_fwd_cross.1 = (bf16[448,768]{1,0:T(8,128)(2,1)S(1)}, bf16[12,448,1536]{2,1,0:T(8,128)(2,1)}, f32[448,768]{1,0:T(8,128)S(1)}) custom-call(s32[1]{0:T(128)S(6)} %copy.44.length_ref, bf16[448,768]{1,0:T(8,128)(2,1)S(1)} %fusion.33.q_ref, bf16[1536,768]{1,0:T(8,128)(2,1)S(1)} %copy-done.16, bf16[1536,768]{1,0:T(8,128)(2,1)S(1)} %copy-done.18), custom_call_target="tpu_custom_call" | custom-call | flops 6341787648 | bytes 16515072 | tf_op jit(solution)/shard_map/attend_fwd_cross/pallas_call | solution.py:88
  128.9 6.8 %multiply_convert_fusion = (bf16[448,1536]{1,0:T(8,128)(2,1)S(1)}, f32[448,1536]{1,0:T(8,128)S(1)}, f32[448,1536]{1,0:T(8,128)S(1)}) fusion(f32[1536]{0:T(1024)S(1)} %copy-done.58, bf16[768,1536]{1,0:T(8,128)(2,1)S(1)} %copy-done, f32[448,768]{1,0:T(8,128)S(1)} %get-tuple-element.161, f32[768]{0:T(1024)S(1)} %get-tuple-element.101, ...), kind=kOutput, calls=%fused_computation.15 | convolution fusion | flops 1104101376 | bytes 10632704 | tf_op jit(solution)/shard_map/dot_general | solution.py:22
  144.6 28.9 %collective-permute-done.3 = f32[448,768]{1,0:T(8,128)} collective-permute-done((f32[448,768]{1,0:T(8,128)}, f32[448,768]{1,0:T(8,128)}, u32[]{:S(2)}, u32[]{:S(2)}) %collective-permute-start.3) | collective-permute-done | bytes 1376288 | tf_op jit(solution)/shard_map/ppermute | solution.py:214
  175.9 26.4 %collective-permute-done.2 = f32[448,768]{1,0:T(8,128)} collective-permute-done((f32[448,768]{1,0:T(8,128)}, f32[448,768]{1,0:T(8,128)}, u32[]{:S(2)}, u32[]{:S(2)}) %collective-permute-start.2) | collective-permute-done | bytes 1376288 | tf_op jit(solution)/shard_map/ppermute | solution.py:214
  202.5 3.5 fusion.90
  207.9 19.6 %attend_bwd.2 = (bf16[448,768]{1,0:T(8,128)(2,1)S(1)}, bf16[768,1536]{1,0:T(8,128)(2,1)S(1)}, bf16[768,1536]{1,0:T(8,128)(2,1)S(1)}) custom-call(bf16[448,768]{1,0:T(8,128)(2,1)S(1)} %copy-done.15, bf16[1536,768]{1,0:T(8,128)(2,1)S(1)} %copy-done.17, bf16[1536,768]{1,0:T(8,128)(2,1)S(1)} %copy-done.19, bf16[12,448,1536]{2,1,0:T(8,128)(2,1)} %get-tuple-element.29.weights_ref, ...), custom_call_target="tpu_custom_call" | custom-call | flops 12683575296 | bytes 16515072 | tf_op jit(solution)/shard_map/attend_bwd/pallas_call | solution.py:153
  240.6 3.7 attend_bwd.3
  254.0 23.8 %collective-permute-done.11 = f32[2,2,1,1,192,384]{5,4,3,2,1,0:T(8,128)S(1)} collective-permute-done((f32[2,2,1,1,192,384]{5,4,3,2,1,0:T(8,128)S(1)}, f32[2,2,1,1,192,384]{5,4,3,2,1,0:T(8,128)S(1)}, u32[]{:S(2)}, u32[]{:S(2)}) %collective-permute-start.11) | collective-permute-done | bytes 1179680 | tf_op jit(solution)/shard_map/ppermute | solution.py:238
  279.8 12.8 %collective-permute-done.12 = f32[2,1,1,1,192,384]{5,4,3,2,1,0:T(8,128)S(1)} collective-permute-done((f32[2,1,1,1,192,384]{5,4,3,2,1,0:T(8,128)S(1)}, f32[2,1,1,1,192,384]{5,4,3,2,1,0:T(8,128)S(1)}, u32[]{:S(2)}, u32[]{:S(2)}) %collective-permute-start.12) | collective-permute-done | bytes 589856 | tf_op jit(solution)/shard_map/ppermute | solution.py:238
  296.3 11.3 %collective-permute-done.13 = f32[1,1,1,1,192,384]{5,4,3,2,1,0:T(8,128)S(1)} collective-permute-done((f32[1,1,1,1,192,384]{5,4,3,2,1,0:T(8,128)S(1)}, f32[1,1,1,1,192,384]{5,4,3,2,1,0:T(8,128)S(1)}, u32[]{:S(2)}, u32[]{:S(2)}) %collective-permute-start.13) | collective-permute-done | bytes 294944 | tf_op jit(solution)/shard_map/ppermute | solution.py:238
  308.6 4.1 constant_dynamic-slice_fusion.22
  312.8 3.6 fusion.88
  333.6 35.7 %collective-permute-done.7 = f32[2,2,1,1,200,384]{5,4,3,2,1,0:T(8,128)S(1)} collective-permute-done((f32[2,2,1,1,200,384]{5,4,3,2,1,0:T(8,128)S(1)}, f32[2,2,1,1,200,384]{5,4,3,2,1,0:T(8,128)S(1)}, u32[]{:S(2)}, u32[]{:S(2)}) %collective-permute-start.7) | collective-permute-done | bytes 1228832 | tf_op jit(solution)/shard_map/ppermute | solution.py:238
  372.2 12.5 %collective-permute-done.8 = f32[2,1,1,1,200,384]{5,4,3,2,1,0:T(8,128)S(1)} collective-permute-done((f32[2,1,1,1,200,384]{5,4,3,2,1,0:T(8,128)S(1)}, f32[2,1,1,1,200,384]{5,4,3,2,1,0:T(8,128)S(1)}, u32[]{:S(2)}, u32[]{:S(2)}) %collective-permute-start.8) | collective-permute-done | bytes 614432 | tf_op jit(solution)/shard_map/ppermute | solution.py:238
  385.8 14.2 %collective-permute-done.9 = f32[1,1,1,1,200,384]{5,4,3,2,1,0:T(8,128)S(1)} collective-permute-done((f32[1,1,1,1,200,384]{5,4,3,2,1,0:T(8,128)S(1)}, f32[1,1,1,1,200,384]{5,4,3,2,1,0:T(8,128)S(1)}, u32[]{:S(2)}, u32[]{:S(2)}) %collective-permute-start.9) | collective-permute-done | bytes 307232 | tf_op jit(solution)/shard_map/ppermute | solution.py:238
  401.3 4.4 maximum_add_fusion
  406.4 69.1 %collective-permute-done.15 = f32[2,2,1,1,192,768]{5,4,3,2,1,0:T(8,128)S(1)} collective-permute-done((f32[2,2,1,1,192,768]{5,4,3,2,1,0:T(8,128)S(1)}, f32[2,2,1,1,192,768]{5,4,3,2,1,0:T(8,128)S(1)}, u32[]{:S(2)}, u32[]{:S(2)}) %collective-permute-start.15) | collective-permute-done | bytes 2359328 | tf_op jit(solution)/shard_map/ppermute | solution.py:238
  476.0 27.0 %collective-permute-done.16 = f32[2,1,1,1,192,768]{5,4,3,2,1,0:T(8,128)S(1)} collective-permute-done((f32[2,1,1,1,192,768]{5,4,3,2,1,0:T(8,128)S(1)}, f32[2,1,1,1,192,768]{5,4,3,2,1,0:T(8,128)S(1)}, u32[]{:S(2)}, u32[]{:S(2)}) %collective-permute-start.16) | collective-permute-done | bytes 1179680 | tf_op jit(solution)/shard_map/ppermute | solution.py:238
  503.2 27.0 %collective-permute-done.17 = f32[1,1,1,1,192,768]{5,4,3,2,1,0:T(8,128)S(1)} collective-permute-done((f32[1,1,1,1,192,768]{5,4,3,2,1,0:T(8,128)S(1)}, f32[1,1,1,1,192,768]{5,4,3,2,1,0:T(8,128)S(1)}, u32[]{:S(2)}, u32[]{:S(2)}) %collective-permute-start.17) | collective-permute-done | bytes 589856 | tf_op jit(solution)/shard_map/ppermute | solution.py:238
  531.2 3.5 fusion.42
  538.8 26.0 %copy.35 = f32[1,1500,768]{2,0,1:T(1,128)} copy(f32[1,1500,768]{2,1,0:T(8,128)S(1)} %fusion) | data formatting | bytes 9216000
  566.1 4.0 slice.305
  571.5 4.0 slice.301
  582.6 26.9 %all-gather.15.cloned.1.call-done = f32[16,1,1,1,192,768]{5,4,3,2,1,0:T(8,128)} async-done(((f32[1,1,1,1,192,768]{5,4,3,2,1,0:T(8,128)}), f32[16,1,1,1,192,768]{5,4,3,2,1,0:T(8,128)}) %all-gather.15.cloned.1.call-update) | async-done | bytes 9437200 | tf_op jit(solution)/shard_map/all_gather | solution.py:244
  (318 shorter events, 121.6 us)
Async XLA Ops:
  7.2 121.6 %copy-start = (bf16[768,1536]{1,0:T(8,128)(2,1)S(1)}, bf16[768,1536]{1,0:T(8,128)(2,1)}, u32[]{:S(2)}) copy-start(bf16[768,1536]{1,0:T(8,128)(2,1)} %param.32) | copy-start | bytes 7077892
  7.2 70.5 %all-gather.9.cloned.1.call-start = ((), (), s32[]{:S(2)}) async-start(), calls=%async_computation | async-start | bytes 5013504 | tf_op jit(solution)/shard_map/all_gather | solution.py:311
  11.1 10.3 %collective-permute-start.1 = (f32[194,384]{1,0:T(8,128)S(1)}, f32[194,384]{1,0:T(8,128)S(1)}, u32[]{:S(2)}, u32[]{:S(2)}) collective-permute-start(f32[194,384]{1,0:T(8,128)S(1)} %pad_maximum_fusion.10), channel_id=1, source_target_pairs={{0,1},{1,0},{2,3},{3,2},{4,5},{5,4},{6,7},{7,6},{8,9},{9,8},{10,11... | collective-permute-start | bytes 893960 | tf_op jit(solution)/shard_map/ppermute | solution.py:214
  22.9 543.2 %all-gather.13.cloned.1.call-start = ((), (), s32[]{:S(2)}) async-start(), calls=%async_computation.2 | async-start | bytes 5013504 | tf_op jit(solution)/shard_map/all_gather | solution.py:244
  31.5 35.5 %copy-start.12 = (f32[448,384]{1,0:T(8,128)}, f32[448,384]{1,0:T(8,128)S(1)}, u32[]{:S(2)}) copy-start(f32[448,384]{1,0:T(8,128)S(1)} %get-tuple-element.33.inverse_ref) | copy-start | bytes 2064388
  33.1 31.7 %collective-permute-start = (f32[448,768]{1,0:T(8,128)}, f32[448,768]{1,0:T(8,128)}, u32[]{:S(2)}, u32[]{:S(2)}) collective-permute-start(f32[448,768]{1,0:T(8,128)} %fusion.45), channel_id=1, source_target_pairs={{0,1},{1,0},{2,3},{3,2},{4,5},{5,4},{6,7},{7,6},{8,9},{9,8},{10,11... | collective-permute-start | bytes 4128776 | tf_op jit(solution)/shard_map/ppermute | solution.py:214
  106.8 20.6 %copy-start.14 = (bf16[448,768]{1,0:T(8,128)(2,1)}, bf16[448,768]{1,0:T(8,128)(2,1)S(1)}, u32[]{:S(2)}) copy-start(bf16[448,768]{1,0:T(8,128)(2,1)S(1)} %fusion.33.q_ref) | copy-start | bytes 2064388
  106.8 20.6 %copy-start.27 = (f32[448,768]{1,0:T(8,128)S(1)}, f32[448,768]{1,0:T(8,128)}, u32[]{:S(2)}) copy-start(f32[448,768]{1,0:T(8,128)} %copy-done.26) | copy-start | bytes 4128772
  106.8 20.6 %copy-start.37 = (bf16[1,768,768]{2,1,0:T(8,128)(2,1)S(1)}, bf16[1,768,768]{2,1,0:T(8,128)(2,1)}, u32[]{:S(2)}) copy-start(bf16[1,768,768]{2,1,0:T(8,128)(2,1)} %join_halves.3) | copy-start | bytes 3538948
  140.1 33.3 %collective-permute-start.3 = (f32[448,768]{1,0:T(8,128)}, f32[448,768]{1,0:T(8,128)}, u32[]{:S(2)}, u32[]{:S(2)}) collective-permute-start(f32[448,768]{1,0:T(8,128)} %fusion.107), channel_id=1, source_target_pairs={{0,1},{1,0},{2,3},{3,2},{4,5},{5,4},{6,7},{7,6},{8,9},{9,8},{10,11... | collective-permute-start | bytes 4128776 | tf_op jit(solution)/shard_map/ppermute | solution.py:214
  141.6 31.9 %copy-start.30 = (f32[448,768]{1,0:T(8,128)S(1)}, f32[448,768]{1,0:T(8,128)}, u32[]{:S(2)}) copy-start(f32[448,768]{1,0:T(8,128)} %copy-done.29) | copy-start | bytes 4128772
  144.0 58.3 %collective-permute-start.2 = (f32[448,768]{1,0:T(8,128)}, f32[448,768]{1,0:T(8,128)}, u32[]{:S(2)}, u32[]{:S(2)}) collective-permute-start(f32[448,768]{1,0:T(8,128)} %fusion.106), channel_id=1, source_target_pairs={{0,1},{1,0},{2,3},{3,2},{4,5},{5,4},{6,7},{7,6},{8,9},{9,8},{10,11... | collective-permute-start | bytes 4128776 | tf_op jit(solution)/shard_map/ppermute | solution.py:214
  144.6 57.7 %copy-start.46 = (bf16[448,768]{1,0:T(8,128)(2,1)S(1)}, bf16[448,768]{1,0:T(8,128)(2,1)}, u32[]{:S(2)}) copy-start(bf16[448,768]{1,0:T(8,128)(2,1)} %param.23) | copy-start | bytes 2064388
  144.6 57.7 %copy-start.53 = (f32[768]{0:T(1024)S(1)}, f32[768]{0:T(1024)}, u32[]{:S(2)}) copy-start(f32[768]{0:T(1024)} %param.35) | copy-start | bytes 9220
  237.3 11.9 %collective-permute-start.10 = (f32[2,2,2,1,192,384]{5,4,3,2,1,0:T(8,128)S(1)}, f32[2,2,2,1,192,384]{5,4,3,2,1,0:T(8,128)S(1)}, u32[]{:S(2)}, u32[]{:S(2)}) collective-permute-start(f32[2,2,2,1,192,384]{5,4,3,2,1,0:T(8,128)S(1)} %pad_maximum_fusion.6), channel_id=1, source_target_pairs={{0,2},{2,0},{4,6},{6,4},{8,10},{10,8},{12,14},{14,12},{16,18},{18,... | collective-permute-start | bytes 7077896 | tf_op jit(solution)/shard_map/ppermute | solution.py:238
  247.1 65.7 %collective-permute-start.4 = (f32[448,768]{1,0:T(8,128)}, f32[448,768]{1,0:T(8,128)}, u32[]{:S(2)}, u32[]{:S(2)}) collective-permute-start(f32[448,768]{1,0:T(8,128)} %convolution_add_fusion.3), channel_id=1, source_target_pairs={{0,1},{1,0},{2,3},{3,2},{4,5},{5,4},{6,7},{7,6},{8,9},{9,8},{10,11... | collective-permute-start | bytes 4128776 | tf_op jit(solution)/shard_map/ppermute | solution.py:214
  249.6 28.1 %collective-permute-start.11 = (f32[2,2,1,1,192,384]{5,4,3,2,1,0:T(8,128)S(1)}, f32[2,2,1,1,192,384]{5,4,3,2,1,0:T(8,128)S(1)}, u32[]{:S(2)}, u32[]{:S(2)}) collective-permute-start(f32[2,2,1,1,192,384]{5,4,3,2,1,0:T(8,128)S(1)} %constant_dynamic-slice_fusion.9), channel_id=1, source_target_pairs={{0,4},{2,6},{4,0},{6,2},{8,12},{10,14},{12,8},{14,10},{16,20},{18,... | collective-permute-start | bytes 3538952 | tf_op jit(solution)/shard_map/ppermute | solution.py:238
  277.9 14.8 %collective-permute-start.12 = (f32[2,1,1,1,192,384]{5,4,3,2,1,0:T(8,128)S(1)}, f32[2,1,1,1,192,384]{5,4,3,2,1,0:T(8,128)S(1)}, u32[]{:S(2)}, u32[]{:S(2)}) collective-permute-start(f32[2,1,1,1,192,384]{5,4,3,2,1,0:T(8,128)S(1)} %constant_dynamic-slice_fusion.8), channel_id=1, source_target_pairs={{0,8},{2,10},{4,12},{6,14},{8,0},{10,2},{12,4},{14,6},{16,24},{18,... | collective-permute-start | bytes 1769480 | tf_op jit(solution)/shard_map/ppermute | solution.py:238
  292.8 14.8 %collective-permute-start.13 = (f32[1,1,1,1,192,384]{5,4,3,2,1,0:T(8,128)S(1)}, f32[1,1,1,1,192,384]{5,4,3,2,1,0:T(8,128)S(1)}, u32[]{:S(2)}, u32[]{:S(2)}) collective-permute-start(f32[1,1,1,1,192,384]{5,4,3,2,1,0:T(8,128)S(1)} %constant_dynamic-slice_fusion.7), channel_id=1, source_target_pairs={{0,16},{2,18},{4,20},{6,22},{8,24},{10,26},{12,28},{14,30},{16,0},... | collective-permute-start | bytes 884744 | tf_op jit(solution)/shard_map/ppermute | solution.py:238
  308.3 263.2 %all-gather.11.cloned.1.call-start = ((), (), s32[]{:S(2)}) async-start(), calls=%async_computation.1 | async-start | bytes 5222400 | tf_op jit(solution)/shard_map/all_gather | solution.py:244
  316.4 3.7 collective-permute-start.5
  322.4 4.7 collective-permute-start.6
  327.5 41.8 %collective-permute-start.7 = (f32[2,2,1,1,200,384]{5,4,3,2,1,0:T(8,128)S(1)}, f32[2,2,1,1,200,384]{5,4,3,2,1,0:T(8,128)S(1)}, u32[]{:S(2)}, u32[]{:S(2)}) collective-permute-start(f32[2,2,1,1,200,384]{5,4,3,2,1,0:T(8,128)S(1)} %constant_dynamic-slice_fusion.16), channel_id=1, source_target_pairs={{0,4},{2,6},{4,0},{6,2},{8,12},{10,14},{12,8},{14,10},{16,20},{18,... | collective-permute-start | bytes 3686408 | tf_op jit(solution)/shard_map/ppermute | solution.py:238
  369.4 15.2 %collective-permute-start.8 = (f32[2,1,1,1,200,384]{5,4,3,2,1,0:T(8,128)S(1)}, f32[2,1,1,1,200,384]{5,4,3,2,1,0:T(8,128)S(1)}, u32[]{:S(2)}, u32[]{:S(2)}) collective-permute-start(f32[2,1,1,1,200,384]{5,4,3,2,1,0:T(8,128)S(1)} %constant_dynamic-slice_fusion.15), channel_id=1, source_target_pairs={{0,8},{2,10},{4,12},{6,14},{8,0},{10,2},{12,4},{14,6},{16,24},{18,... | collective-permute-start | bytes 1843208 | tf_op jit(solution)/shard_map/ppermute | solution.py:238
  372.2 29.1 %collective-permute-start.14 = (f32[2,2,2,1,192,768]{5,4,3,2,1,0:T(8,128)}, f32[2,2,2,1,192,768]{5,4,3,2,1,0:T(8,128)}, u32[]{:S(2)}, u32[]{:S(2)}) collective-permute-start(f32[2,2,2,1,192,768]{5,4,3,2,1,0:T(8,128)} %pad_maximum_fusion.1), channel_id=1, source_target_pairs={{0,2},{2,0},{4,6},{6,4},{8,10},{10,8},{12,14},{14,12},{16,18},{18,... | collective-permute-start | bytes 14155784 | tf_op jit(solution)/shard_map/ppermute | solution.py:238
  384.8 15.2 %collective-permute-start.9 = (f32[1,1,1,1,200,384]{5,4,3,2,1,0:T(8,128)S(1)}, f32[1,1,1,1,200,384]{5,4,3,2,1,0:T(8,128)S(1)}, u32[]{:S(2)}, u32[]{:S(2)}) collective-permute-start(f32[1,1,1,1,200,384]{5,4,3,2,1,0:T(8,128)S(1)} %constant_dynamic-slice_fusion.14), channel_id=1, source_target_pairs={{0,16},{2,18},{4,20},{6,22},{8,24},{10,26},{12,28},{14,30},{16,0},... | collective-permute-start | bytes 921608 | tf_op jit(solution)/shard_map/ppermute | solution.py:238
  400.8 208.7 %all-gather.15.cloned.1.call-start = ((), (), s32[]{:S(2)}) async-start(), calls=%async_computation.3 | async-start | bytes 10027008 | tf_op jit(solution)/shard_map/all_gather | solution.py:244
  405.8 69.6 %collective-permute-start.15 = (f32[2,2,1,1,192,768]{5,4,3,2,1,0:T(8,128)S(1)}, f32[2,2,1,1,192,768]{5,4,3,2,1,0:T(8,128)S(1)}, u32[]{:S(2)}, u32[]{:S(2)}) collective-permute-start(f32[2,2,1,1,192,768]{5,4,3,2,1,0:T(8,128)S(1)} %constant_dynamic-slice_fusion.2), channel_id=1, source_target_pairs={{0,4},{2,6},{4,0},{6,2},{8,12},{10,14},{12,8},{14,10},{16,20},{18,... | collective-permute-start | bytes 7077896 | tf_op jit(solution)/shard_map/ppermute | solution.py:238
  475.9 27.1 %collective-permute-start.16 = (f32[2,1,1,1,192,768]{5,4,3,2,1,0:T(8,128)S(1)}, f32[2,1,1,1,192,768]{5,4,3,2,1,0:T(8,128)S(1)}, u32[]{:S(2)}, u32[]{:S(2)}) collective-permute-start(f32[2,1,1,1,192,768]{5,4,3,2,1,0:T(8,128)S(1)} %constant_dynamic-slice_fusion.1), channel_id=1, source_target_pairs={{0,8},{2,10},{4,12},{6,14},{8,0},{10,2},{12,4},{14,6},{16,24},{18,... | collective-permute-start | bytes 3538952 | tf_op jit(solution)/shard_map/ppermute | solution.py:238
  503.2 27.1 %collective-permute-start.17 = (f32[1,1,1,1,192,768]{5,4,3,2,1,0:T(8,128)S(1)}, f32[1,1,1,1,192,768]{5,4,3,2,1,0:T(8,128)S(1)}, u32[]{:S(2)}, u32[]{:S(2)}) collective-permute-start(f32[1,1,1,1,192,768]{5,4,3,2,1,0:T(8,128)S(1)} %constant_dynamic-slice_fusion), channel_id=1, source_target_pairs={{0,16},{2,18},{4,20},{6,22},{8,24},{10,26},{12,28},{14,30},{16,0},... | collective-permute-start | bytes 1769480 | tf_op jit(solution)/shard_map/ppermute | solution.py:238
  538.8 26.0 %copy-start.25 = (f32[448,768]{1,0:T(8,128)S(1)}, f32[448,768]{1,0:T(8,128)}, u32[]{:S(2)}) copy-start(f32[448,768]{1,0:T(8,128)} %copy-done.24) | copy-start | bytes 4128772
  538.8 26.0 %copy-start.36 = (f32[448,768]{1,0:T(8,128)S(1)}, f32[448,768]{1,0:T(8,128)}, u32[]{:S(2)}) copy-start(f32[448,768]{1,0:T(8,128)} %get-tuple-element.114) | copy-start | bytes 4128772
  (54 other events, 257.8 us)
Sparse Core Ops, SparseCore 0:
  23.0 54.6 all-gather.8
  308.4 63.7 all-gather.12
  400.9 68.3 all-gather.10
  531.3 78.1 all-gather.14

commit v2 on v1

v2 whole, which is shorter than its diff:
```python
from functools import partial

import jax
import jax.numpy as jnp
from jax import lax
from jax.experimental import pallas as pl
from jax.experimental.pallas import tpu as pltpu
from jax.sharding import PartitionSpec as P

HEAD_DIM = 64
SCALE = HEAD_DIM ** (-0.5)
PAIR = 2 * HEAD_DIM
FF_BLOCK = 256
FRAME_BLOCK = 256
VMEM_LIMIT = 58 * 1024 * 1024
COST_SHARE = 64
epsilon = 1e-05
masked_value = -1e30
f32 = jnp.float32
bf16 = jnp.bfloat16


def dot(a, b, ca, cb):
    return lax.dot_general(a, b, (((ca,), (cb,)), ((), ())), preferred_element_type=f32)


def shaped(shape, dtype):
    return jax.ShapeDtypeStruct(shape, dtype)


class Source:
    def __init__(self, ref, held, sems, first_sem, pieces):
        self.held, self.shape, self.dtype = held, held.shape, held.dtype
        self.size = held.shape[0] // pieces
        self.ref, self.sems, self.first_sem = ref, sems, first_sem
        self.copies = [None] * pieces
        self.pending = [True] * pieces

    def fetch(self, *pieces):
        for piece in pieces or range(len(self.copies)):
            if self.copies[piece] is None:
                here = pl.ds(piece * self.size, self.size)
                self.copies[piece] = pltpu.make_async_copy(
                    self.ref.at[here], self.held.at[here], self.sems.at[self.first_sem + piece]
                )
                self.copies[piece].start()

    def wait(self, piece):
        if self.pending[piece]:
            self.fetch(piece)
            self.pending[piece] = False
            self.copies[piece].wait()

    def __getitem__(self, index):
        if len(self.copies) > 1 and isinstance(index, int):
            self.wait(index // self.size)
        else:
            for piece in range(len(self.copies)):
                self.wait(piece)
        return self.held[index]


class Sink:
    def __init__(self, ref, held, sems, first_sem, pieces):
        self.held, self.shape, self.dtype = held, held.shape, held.dtype
        self.size = held.shape[0] // pieces
        self.copies = []
        self.sent = []
        for i in range(pieces):
            here = pl.ds(i * self.size, self.size)
            self.copies.append(pltpu.make_async_copy(held.at[here], ref.at[here], sems.at[first_sem + i]))
            self.sent.append(False)

    def __getitem__(self, index):
        return self.held[index]

    def __setitem__(self, index, value):
        self.held[index] = value

    def send(self, piece=0):
        self.sent[piece] = True
        self.copies[piece].start()


def call(kernel, name, out_shape, flops, early, scalars, *arrays):
    arrays = [a if isinstance(a, tuple) else (a, 1) for a in arrays]
    outs = [o if isinstance(o, tuple) else (o, 1) for o in out_shape]
    in_pieces = [pieces for _, pieces in arrays]
    out_pieces = [pieces for _, pieces in outs]
    arrays = [a for a, _ in arrays]
    outs = [o for o, _ in outs]
    moved = sum(a.size * a.dtype.itemsize for a in (*arrays, *outs))

    def body(*refs):
        refs = list(refs)
        scalar_refs = [refs.pop(0) for _ in scalars]
        in_refs = [refs.pop(0) for _ in arrays]
        out_refs = [refs.pop(0) for _ in outs]
        in_held = [refs.pop(0) for _ in arrays]
        out_held = [refs.pop(0) for _ in outs]
        in_sems, out_sems = refs
        sources = []
        for i, (ref, held) in enumerate(zip(in_refs, in_held)):
            sources.append(Source(ref, held, in_sems, sum(in_pieces[:i]), in_pieces[i]))
        sinks = []
        for i, (ref, held) in enumerate(zip(out_refs, out_held)):
            sinks.append(Sink(ref, held, out_sems, sum(out_pieces[:i]), out_pieces[i]))
        for source in sources[:early]:
            source.fetch()
        kernel(*scalar_refs, *sources, *sinks)
        for source in sources:
            for piece in range(len(source.copies)):
                if source.copies[piece] is not None:
                    source.wait(piece)
        for sink in sinks:
            for piece, sent in enumerate(sink.sent):
                if not sent:
                    sink.send(piece)
        for sink in sinks:
            for copy in sink.copies:
                copy.wait()

    anywhere = pl.BlockSpec(memory_space=pl.ANY)
    return pl.pallas_call(
        body,
        in_specs=[pl.BlockSpec(memory_space=pltpu.SMEM)] * len(scalars) + [anywhere] * len(arrays),
        out_specs=[anywhere] * len(outs),
        out_shape=outs,
        scratch_shapes=[pltpu.VMEM(a.shape, a.dtype) for a in (*arrays, *outs)]
        + [pltpu.SemaphoreType.DMA((sum(in_pieces),)), pltpu.SemaphoreType.DMA((sum(out_pieces),))],
        compiler_params=pltpu.CompilerParams(vmem_limit_bytes=VMEM_LIMIT),
        cost_estimate=pl.CostEstimate(flops=flops // COST_SHARE, bytes_accessed=moved // COST_SHARE, transcendentals=0),
        name=name,
    )(*scalars, *arrays)


def lanes_of(pair):
    return slice(pair * PAIR, (pair + 1) * PAIR)


def add_up(terms):
    total = terms[0]
    for term in terms[1:]:
        total = total + term
    return total


def norm_unit(values):
    centered = values - jnp.mean(values, axis=-1, keepdims=True)
    inverse = lax.rsqrt(jnp.mean(centered * centered, axis=-1, keepdims=True) + epsilon)
    return centered * inverse, inverse


def norm_backward(incoming, unit, inverse, gain):
    scaled = incoming * gain
    scaled_mean = jnp.mean(scaled, axis=-1, keepdims=True)
    along_unit = jnp.mean(scaled * unit, axis=-1, keepdims=True)
    return inverse * (scaled - scaled_mean - unit * along_unit)


def column_sum(values):
    return jnp.sum(values, axis=0, keepdims=True)


def live_gradient(cotangent, text_len, corpus_weight):
    places = lax.broadcasted_iota(jnp.int32, (cotangent.shape[0], 1), 0)
    live = jnp.where(places < text_len, corpus_weight, 0.0)
    return cotangent.astype(f32) * live


def lane_masks(rows):
    return lax.broadcasted_iota(jnp.int32, (rows, PAIR), 1) < HEAD_DIM


def pair_forward(length, causal, q, k, v, weights_ref, start):
    rows, columns = q.shape[0], k.shape[0]
    first_lanes = lane_masks(rows)
    if causal:
        places = lax.broadcasted_iota(jnp.int32, (rows, columns), 1)
        allowed = (places < length) & (places <= lax.broadcasted_iota(jnp.int32, (rows, columns), 0))
    else:
        places = lax.broadcasted_iota(jnp.int32, (1, columns), 1)
        shift = jnp.where(places < length, 0.0, masked_value)
    scores = []
    for head in range(2):
        mine = first_lanes if head == 0 else jnp.logical_not(first_lanes)
        raw = dot(jnp.where(mine, q, jnp.zeros_like(q)), k, 1, 1)
        scores.append(jnp.where(allowed, raw, masked_value) if causal else raw + shift)
    inverses = []
    for head in range(2):
        largest = jnp.max(scores[head], axis=-1, keepdims=True)
        weights = jnp.exp(scores[head] - largest)
        inverses.append(1.0 / jnp.sum(weights, axis=-1, keepdims=True))
        weights_ref[start + head] = weights.astype(bf16)
    mixed = [dot(weights_ref[start + head], v, 1, 0) for head in range(2)]
    inverse = jnp.where(first_lanes, inverses[0], inverses[1])
    return (jnp.where(first_lanes, mixed[0], mixed[1]) * inverse).astype(bf16), inverse


def pair_backward(q, k, v, weights_ref, start, inverse, heads, grad_heads):
    first_lanes = lane_masks(q.shape[0])
    grad = (grad_heads.astype(f32) * inverse).astype(bf16)
    along = grad.astype(f32) * heads.astype(f32)
    dq = []
    dk = None
    dv = None
    for head in range(2):
        mine = first_lanes if head == 0 else jnp.logical_not(first_lanes)
        grad_one = jnp.where(mine, grad, jnp.zeros_like(grad))
        q_one = jnp.where(mine, q, jnp.zeros_like(q))
        row_terms = jnp.sum(jnp.where(mine, along, 0.0), axis=-1, keepdims=True)
        weights = weights_ref[start + head]
        grad_probs = dot(grad_one, v, 1, 1)
        grad_scores = (weights.astype(f32) * (grad_probs - row_terms)).astype(bf16)
        dv_one = dot(grad_one, weights, 0, 0)
        dk_one = dot(q_one, grad_scores, 0, 0)
        dq.append(dot(grad_scores, k, 1, 0))
        dk = dk_one if dk is None else dk + dk_one
        dv = dv_one if dv is None else dv + dv_one
    dq = (jnp.where(first_lanes, dq[0], dq[1]) * SCALE).astype(bf16)
    return dq, dk.astype(bf16), dv.astype(bf16)


def row_sums(values):
    return dot(jnp.ones((8, values.shape[1]), bf16), values, 1, 1)


def self_forward_kernel(
    length_ref, hidden_ref, gain_ref, shift_ref, proj_ref, bias_ref, out_ref,
    normed_ref, q_ref, k_ref, v_ref, weights_ref, inverse_ref, heads_ref, partial_ref,
):
    unit, _ = norm_unit(hidden_ref[...].astype(f32))
    normed = (unit * gain_ref[0:1, :] + shift_ref[0:1, :]).astype(bf16)
    normed_ref[...] = normed
    normed_ref.send()
    out_ref.fetch(0)
    q_ref[...] = ((dot(normed, proj_ref[0], 1, 0) + bias_ref[0:1]) * SCALE).astype(bf16)
    k_ref[...] = dot(normed, proj_ref[1], 1, 0).astype(bf16)
    v_ref[...] = (dot(normed, proj_ref[2], 1, 0) + bias_ref[1:2]).astype(bf16)
    q_ref.send()
    k_ref.send()
    v_ref.send()
    for pair in range(q_ref.shape[1] // PAIR):
        lanes = lanes_of(pair)
        heads, inverse = pair_forward(
            length_ref[0], True, q_ref[:, lanes], k_ref[:, lanes], v_ref[:, lanes], weights_ref, 2 * pair
        )
        weights_ref.send(pair)
        heads_ref[:, lanes] = heads
        inverse_ref[:, lanes] = inverse
    heads_ref.send()
    inverse_ref.send()
    partial_ref[...] = dot(heads_ref[...], out_ref[0], 1, 0)


def self_forward(text_len, hidden, gain, shift, proj, bias, out_proj):
    rows, width = hidden.shape
    half = proj.shape[2]
    return call(
        self_forward_kernel,
        "self_forward",
        [
            shaped((rows, width), bf16),
            shaped((rows, half), bf16),
            shaped((rows, half), bf16),
            shaped((rows, half), bf16),
            (shaped((half // HEAD_DIM, rows, rows), bf16), half // PAIR),
            shaped((rows, half), f32),
            shaped((rows, half), bf16),
            shaped((rows, width), f32),
        ],
        8 * rows * width * half + 12 * rows * rows * half,
        6,
        (text_len,),
        hidden, gain, shift, (proj, 3), bias, (out_proj, 2),
    )


def cross_own_kernel(
    length_ref, received_ref, partial_ref, hidden_ref, out_bias_ref, gain_ref, shift_ref,
    proj_ref, bias_ref, k_ref, v_ref, out_ref,
    first_ref, normed_ref, q_ref, weights_ref, inverse_ref, heads_ref, term_ref,
):
    first = hidden_ref[...].astype(f32) + (partial_ref[...] + received_ref[...]) + out_bias_ref[0:1, :]
    first_ref[...] = first
    first_ref.send()
    proj_ref.fetch(0)
    bias_ref.fetch()
    k_ref.fetch()
    v_ref.fetch()
    out_ref.fetch(1)
    unit, _ = norm_unit(first)
    normed = (unit * gain_ref[1:2, :] + shift_ref[1:2, :]).astype(bf16)
    normed_ref[...] = normed
    normed_ref.send()
    q_ref[...] = ((dot(normed, proj_ref[0], 1, 0) + bias_ref[0:1]) * SCALE).astype(bf16)
    q_ref.send()
    for pair in range(q_ref.shape[1] // PAIR):
        lanes = lanes_of(pair)
        heads, inverse = pair_forward(
            length_ref[0], False, q_ref[:, lanes], k_ref[:, lanes], v_ref[:, lanes], weights_ref, 2 * pair
        )
        weights_ref.send(pair)
        heads_ref[:, lanes] = heads
        inverse_ref[:, lanes] = inverse
    heads_ref.send()
    inverse_ref.send()
    term_ref[...] = dot(heads_ref[...], out_ref[1], 1, 0)


def cross_own(audio_len, hidden, partial_self, received, out_bias, gain, shift, proj, bias, k, v, out_proj):
    rows, width = hidden.shape
    columns, half = k.shape
    return call(
        cross_own_kernel,
        "cross_own",
        [
            shaped((rows, width), f32),
            shaped((rows, width), bf16),
            shaped((rows, half), bf16),
            (shaped((half // HEAD_DIM, rows, columns), bf16), half // PAIR),
            shaped((rows, half), f32),
            shaped((rows, half), bf16),
            shaped((rows, width), f32),
        ],
        4 * rows * width * half + 12 * rows * columns * half,
        6,
        (audio_len,),
        received, partial_self, hidden, out_bias, gain, shift, (proj, 3), bias, k, v, (out_proj, 2),
    )


def cross_other_kernel(
    length_ref, gathered_ref, normed_ref, frames_ref, bias_ref,
    q_ref, k_ref, v_ref, weights_ref, inverse_ref, heads_ref, term_ref, wq_ref, wk_ref, wv_ref, wo_ref,
):
    width, half = wq_ref.shape
    for i, ref in enumerate((wq_ref, wk_ref, wv_ref)):
        ref[...] = gathered_ref[i * width : (i + 1) * width, :].astype(bf16)
        ref.send()
    for i in range(width // half):
        start = 3 * width + i * half
        wo_ref[:, i * half : (i + 1) * half] = gathered_ref[start : start + half, :].astype(bf16)
    wo_ref.send()
    q_ref[...] = ((dot(normed_ref[...], wq_ref[...], 1, 0) + bias_ref[0:1]) * SCALE).astype(bf16)
    k_ref[...] = dot(frames_ref[...], wk_ref[...], 1, 0).astype(bf16)
    v_ref[...] = (dot(frames_ref[...], wv_ref[...], 1, 0) + bias_ref[1:2]).astype(bf16)
    q_ref.send()
    k_ref.send()
    v_ref.send()
    for pair in range(half // PAIR):
        lanes = lanes_of(pair)
        heads, inverse = pair_forward(
            length_ref[0], False, q_ref[:, lanes], k_ref[:, lanes], v_ref[:, lanes], weights_ref, 2 * pair
        )
        weights_ref.send(pair)
        heads_ref[:, lanes] = heads
        inverse_ref[:, lanes] = inverse
    heads_ref.send()
    inverse_ref.send()
    term_ref[...] = dot(heads_ref[...], wo_ref[...], 1, 0)


def cross_other(audio_len, normed, frames_in, gathered, bias):
    rows, width = normed.shape
    columns = frames_in.shape[0]
    half = gathered.shape[1]
    proj = shaped((width, half), bf16)
    return call(
        cross_other_kernel,
        "cross_other",
        [
            shaped((rows, half), bf16),
            shaped((columns, half), bf16),
            shaped((columns, half), bf16),
            (shaped((half // HEAD_DIM, rows, columns), bf16), half // PAIR),
            shaped((rows, half), f32),
            shaped((rows, half), bf16),
            shaped((rows, width), f32),
            proj,
            proj,
            proj,
            shaped((half, width), bf16),
        ],
        4 * rows * width * half + 4 * columns * width * half + 12 * rows * columns * half,
        4,
        (audio_len,),
        gathered, normed, frames_in, bias,
    )


def error_function(x):
    x = jnp.clip(x, -4.0, 4.0)
    square = x * x
    top = jnp.full_like(x, -2.72614225801306e-10)
    for c in (
        2.77068142495902e-08,
        -2.10102402082508e-06,
        -5.69250639462346e-05,
        -7.34990630326855e-04,
        -2.95459980854025e-03,
        -1.60960333262415e-02,
    ):
        top = top * square + c
    bottom = jnp.full_like(x, -1.45660718464996e-05)
    for c in (-2.13374055278905e-04, -1.68282697438203e-03, -7.37332916720468e-03, -1.42647390514189e-02):
        bottom = bottom * square + c
    return x * top / bottom


def feed_forward_kernel(
    length_ref, weight_ref, own_ref, other_ref, first_ref, out_bias_ref, gain_ref, shift_ref,
    fc1_ref, fc1_bias_ref, cotangent_ref, fc2_ref,
    second_ref, normed_grad_ref, grads_ref, mlp_ref, fc1_bias_grad_ref, fc2_bias_grad_ref,
):
    second = first_ref[...] + (own_ref[...] + other_ref[...]) + out_bias_ref[1:2, :]
    second_ref[...] = second
    second_ref.send()
    for source in (fc1_ref, fc1_bias_ref, cotangent_ref, fc2_ref):
        source.fetch()
    unit, _ = norm_unit(second)
    normed = (unit * gain_ref[2:3, :] + shift_ref[2:3, :]).astype(bf16)
    grad_y = live_gradient(cotangent_ref[...], length_ref[0], weight_ref[0])
    fc2_bias_grad_ref[...] = column_sum(grad_y)
    grad = grad_y.astype(bf16)
    units, width = fc2_ref.shape
    for start in range(0, units, FF_BLOCK):
        here = slice(start, start + FF_BLOCK)
        fc1 = fc1_ref[:, here]
        pre = dot(normed, fc1, 1, 0) + fc1_bias_ref[:, here]
        cdf = 0.5 * (1.0 + error_function(pre * 0.7071067811865476))
        inner = (pre * cdf).astype(bf16)
        slope = cdf + pre * (0.3989422804014327 * jnp.exp(-0.5 * pre * pre))
        fc2 = fc2_ref[here, :]
        grad_pre = (dot(grad, fc2, 1, 1) * slope).astype(bf16)
        fc1_bias_grad_ref[:, here] = column_sum(grad_pre.astype(f32))
        grads_ref[here, :] = dot(inner, grad, 0, 0)
        block = units + (start // width) * width
        grads_ref[block : block + width, start % width : start % width + FF_BLOCK] = dot(normed, grad_pre, 0, 0)
        mlp_term = dot(inner, fc2, 1, 0)
        normed_term = dot(grad_pre, fc1, 1, 1)
        if start == 0:
            mlp_ref[...] = mlp_term
            normed_grad_ref[...] = normed_term
        else:
            mlp_ref[...] += mlp_term
            normed_grad_ref[...] += normed_term
        if (start + FF_BLOCK) % width == 0:
            grads_ref.send(start // width)
            grads_ref.send((units + start) // width)


def feed_forward(text_len, corpus_weight, first, own, other, out_bias, gain, shift, cotangent, fc1, fc1_bias, fc2):
    rows, width = first.shape
    units = fc2.shape[0]
    full = shaped((rows, width), f32)
    return call(
        feed_forward_kernel,
        "feed_forward",
        [
            full,
            full,
            (shaped((2 * units, width), f32), 2 * units // width),
            full,
            shaped((1, units), f32),
            shaped((1, width), f32),
        ],
        12 * rows * width * units,
        6,
        (text_len, corpus_weight),
        own, other, first, out_bias, gain, shift, fc1, fc1_bias, cotangent, fc2,
    )


def projection_grads(core, normed, source, low, dq, dk, dv, heads, theirs_ref, mine_ref):
    part = theirs_ref.shape[1]
    for out_ref, side in ((theirs_ref, 1 - core), (mine_ref, core)):
        here = pl.ds(pl.multiple_of(side * part, PAIR), part)
        piece = source[:, here]
        out_ref[0] = dot(normed[:, here], dq[...], 0, 0)
        out_ref[1] = dot(piece, dk[...], 0, 1)
        out_ref[2] = dot(piece, dv[...], 0, 1)
        out_ref[3] = dot(heads[...], low[:, here], 0, 0)
        out_ref.send()


def cross_own_back_kernel(
    length_ref, weight_ref, core_ref, received_ref, partial_ref, second_ref, cotangent_ref, gain_ref,
    out_ref, q_ref, k_ref, v_ref, inverse_ref, heads_ref, weights_ref, proj_ref, normed_ref, frames_ref,
    grad_second_ref, low_ref, gain_grad_ref, shift_grad_ref, bias_grad_ref,
    dq_ref, dk_ref, dv_ref, term_ref, dq_sum_ref, dv_sum_ref, theirs_ref, mine_ref,
):
    incoming = partial_ref[...] + received_ref[...]
    unit, inverse = norm_unit(second_ref[...])
    gain_grad_ref[...] = column_sum(incoming * unit)
    shift_grad_ref[...] = column_sum(incoming)
    grad_second = live_gradient(cotangent_ref[...], length_ref[0], weight_ref[0]) + norm_backward(
        incoming, unit, inverse, gain_ref[2:3, :]
    )
    grad_second_ref[...] = grad_second
    out_ref.fetch(1)
    for source in (q_ref, k_ref, v_ref, inverse_ref, heads_ref, weights_ref):
        source.fetch()
    proj_ref.fetch(0)
    normed_ref.fetch()
    frames_ref.fetch()
    grad_second_ref.send()
    low = grad_second.astype(bf16)
    low_ref[...] = low
    low_ref.send()
    bias_grad_ref[...] = column_sum(grad_second)
    grad_heads = dot(low, out_ref[1], 1, 1).astype(bf16)
    for pair in range(q_ref.shape[1] // PAIR):
        lanes = lanes_of(pair)
        dq, dk, dv = pair_backward(
            q_ref[:, lanes], k_ref[:, lanes], v_ref[:, lanes], weights_ref, 2 * pair,
            inverse_ref[:, lanes], heads_ref[:, lanes], grad_heads[:, lanes],
        )
        dq_ref[:, lanes] = dq
        dk_ref[lanes, :] = dk
        dv_ref[lanes, :] = dv
    dk_ref.send()
    dv_ref.send()
    projection_grads(
        core_ref[0], normed_ref, frames_ref, low_ref, dq_ref, dk_ref, dv_ref, heads_ref, theirs_ref, mine_ref
    )
    term_ref[...] = dot(dq_ref[...], proj_ref[0], 1, 1)
    dq_sum_ref[...] = column_sum(dq_ref[...].astype(f32))
    dv_sum_ref[...] = row_sums(dv_ref[...])


def cross_own_back(
    text_len, corpus_weight, core, cotangent, second, partial_normed, received, gain, out_proj, proj,
    q, k, v, weights, inverse, heads, normed, frames_in,
):
    rows, width = second.shape
    columns, half = k.shape
    vector = shaped((1, width), f32)
    grads = shaped((4, width // 2, half), f32)
    return call(
        cross_own_back_kernel,
        "cross_own_back",
        [
            shaped((rows, width), f32),
            shaped((rows, width), bf16),
            vector,
            vector,
            vector,
            shaped((rows, half), bf16),
            shaped((half, columns), bf16),
            shaped((half, columns), bf16),
            shaped((rows, width), f32),
            shaped((1, half), f32),
            shaped((8, half), f32),
            grads,
            grads,
        ],
        8 * rows * width * half + 4 * columns * width * half + 24 * rows * columns * half,
        5,
        (text_len, corpus_weight, core),
        received, partial_normed, second, cotangent, gain, (out_proj, 2), q, k, v, inverse, heads,
        (weights, half // PAIR), (proj, 3), normed, frames_in,
    )


def other_back_kernel(
    core_ref, low_in_ref, wo_ref, q_ref, k_ref, v_ref, inverse_ref, heads_ref, weights_ref, wq_ref,
    own_term_ref, first_ref, grad_second_ref, gain_ref,
    out_ref, self_q_ref, self_k_ref, self_v_ref, self_inverse_ref, self_heads_ref, self_weights_ref,
    proj_ref, hidden_ref, normed_ref,
    dk_ref, dv_ref, grad_first_ref, gain_grad_ref, shift_grad_ref, bias_grad_ref,
    term_ref, theirs_ref, mine_ref, self_gain_grad_ref, self_shift_grad_ref, dq_sum_ref, dv_sum_ref,
    low_ref, self_dq_ref, self_dk_ref, self_dv_ref,
):
    grad_heads = dot(low_in_ref[...], wo_ref[...], 1, 1).astype(bf16)
    for source in (wq_ref, own_term_ref, first_ref, grad_second_ref, gain_ref):
        source.fetch()
    out_ref.fetch(0)
    for source in (
        self_q_ref, self_k_ref, self_v_ref, self_inverse_ref, self_heads_ref, self_weights_ref, proj_ref,
        hidden_ref, normed_ref,
    ):
        source.fetch()
    pairs = q_ref.shape[1] // PAIR
    dqs = []
    for pair in range(pairs):
        lanes = lanes_of(pair)
        dq, dk, dv = pair_backward(
            q_ref[:, lanes], k_ref[:, lanes], v_ref[:, lanes], weights_ref, 2 * pair,
            inverse_ref[:, lanes], heads_ref[:, lanes], grad_heads[:, lanes],
        )
        dqs.append(dq)
        dk_ref[lanes, :] = dk
        dv_ref[lanes, :] = dv
    dk_ref.send()
    dv_ref.send()
    incoming = own_term_ref[...] + dot(jnp.concatenate(dqs, axis=1), wq_ref[...], 1, 1)
    unit, inverse = norm_unit(first_ref[...])
    gain_grad_ref[...] = column_sum(incoming * unit)
    shift_grad_ref[...] = column_sum(incoming)
    grad_first = grad_second_ref[...] + norm_backward(incoming, unit, inverse, gain_ref[1:2, :])
    grad_first_ref[...] = grad_first
    grad_first_ref.send()
    low = grad_first.astype(bf16)
    low_ref[...] = low
    bias_grad_ref[...] = column_sum(grad_first)

    grad_heads = dot(low, out_ref[0], 1, 1).astype(bf16)
    for pair in range(pairs):
        lanes = lanes_of(pair)
        dq, dk, dv = pair_backward(
            self_q_ref[:, lanes], self_k_ref[:, lanes], self_v_ref[:, lanes], self_weights_ref, 2 * pair,
            self_inverse_ref[:, lanes], self_heads_ref[:, lanes], grad_heads[:, lanes],
        )
        self_dq_ref[:, lanes] = dq
        self_dk_ref[lanes, :] = dk
        self_dv_ref[lanes, :] = dv
    projection_grads(
        core_ref[0], normed_ref, normed_ref, low_ref, self_dq_ref, self_dk_ref, self_dv_ref, self_heads_ref,
        theirs_ref, mine_ref,
    )
    incoming = dot(self_dq_ref[...], proj_ref[0], 1, 1) + (
        dot(self_dk_ref[...], proj_ref[1], 0, 1) + dot(self_dv_ref[...], proj_ref[2], 0, 1)
    )
    term_ref[...] = incoming
    term_ref.send()
    unit, _ = norm_unit(hidden_ref[...].astype(f32))
    self_gain_grad_ref[...] = column_sum(incoming * unit)
    self_shift_grad_ref[...] = column_sum(incoming)
    dq_sum_ref[...] = column_sum(self_dq_ref[...].astype(f32))
    dv_sum_ref[...] = row_sums(self_dv_ref[...])


def other_back(
    core, low, wo, wq, q, k, v, weights, inverse, heads, own_term, first, grad_second, gain,
    out_proj, proj, self_q, self_k, self_v, self_weights, self_inverse, self_heads, hidden, normed,
):
    rows, width = first.shape
    columns, half = k.shape
    vector = shaped((1, width), f32)
    grads = shaped((4, width // 2, half), f32)
    return call(
        other_back_kernel,
        "other_back",
        [
            shaped((half, columns), bf16),
            shaped((half, columns), bf16),
            shaped((rows, width), f32),
            vector,
            vector,
            vector,
            shaped((rows, width), f32),
            grads,
            grads,
            vector,
            vector,
            shaped((1, half), f32),
            shaped((8, half), f32),
            shaped((rows, width), bf16),
            shaped((rows, half), bf16),
            shaped((half, rows), bf16),
            shaped((half, rows), bf16),
        ],
        20 * rows * width * half + 24 * rows * (columns + rows) * half,
        8,
        (core,),
        low, wo, q, k, v, inverse, heads, (weights, half // PAIR), wq, own_term, first, grad_second, gain,
        (out_proj, 2), self_q, self_k, self_v, self_inverse, self_heads, (self_weights, half // PAIR),
        (proj, 3), hidden, normed,
    )


def encoder_grad_kernel(dk0_ref, dv0_ref, dk1_ref, dv1_ref, proj_ref, wk1_ref, wv1_ref, out_ref):
    own = dot(dk0_ref[...], proj_ref[1], 0, 1) + dot(dv0_ref[...], proj_ref[2], 0, 1)
    other = dot(dk1_ref[...], wk1_ref[...], 0, 1) + dot(dv1_ref[...], wv1_ref[...], 0, 1)
    out_ref[:, 0, :] = own + other


def encoder_grad(dk0, dv0, dk1, dv1, proj, wk1, wv1, frames):
    half, padded = dk0.shape
    width = wk1.shape[0]
    grad_block = pl.BlockSpec((half, FRAME_BLOCK), lambda i: (0, i))
    weight = pl.BlockSpec(wk1.shape, lambda i: (0, 0))
    return pl.pallas_call(
        encoder_grad_kernel,
        grid=(padded // FRAME_BLOCK,),
        in_specs=[grad_block] * 4 + [pl.BlockSpec(proj.shape, lambda i: (0, 0, 0)), weight, weight],
        out_specs=pl.BlockSpec((FRAME_BLOCK, 1, width), lambda i: (i, 0, 0)),
        out_shape=shaped((frames, 1, width), f32),
        compiler_params=pltpu.CompilerParams(vmem_limit_bytes=VMEM_LIMIT),
        cost_estimate=pl.CostEstimate(
            flops=8 * half * padded * width, bytes_accessed=6 * frames * width, transcendentals=0
        ),
        name="encoder_grad",
    )(dk0, dv0, dk1, dv1, proj, wk1, wv1)


def swap(value):
    return lax.ppermute(value, "tensor", [(0, 1), (1, 0)])


def tie(*values):
    return lax.optimization_barrier(values)


class Scatter:
    def __init__(self, theirs, mine):
        self.members = lax.axis_size("dp")
        self.bits = self.members.bit_length() - 1
        self.bit = 0
        self.theirs, self.mine = theirs, mine

    def launch(self):
        if self.bit == self.bits:
            return
        other = 1 << self.bit
        self.received = lax.ppermute(self.theirs, "dp", [(i, i ^ other) for i in range(self.members)])

    def land(self):
        if self.bit == self.bits:
            return
        total = self.mine + self.received
        if self.bit == 0:
            lead = total.shape[:-2]
            self.lead = len(lead)
            cuts = self.bits - 1
            total = total.reshape(lead + (2,) * cuts + (total.shape[-2] >> cuts, total.shape[-1]))
        self.bit += 1
        if self.bit < self.bits:
            axis = self.lead + self.bits - 1 - self.bit
            side = (lax.axis_index("dp") >> self.bit) & 1
            self.mine = lax.dynamic_index_in_dim(total, side, axis, keepdims=True)
            self.theirs = lax.dynamic_index_in_dim(total, 1 - side, axis, keepdims=True)
        else:
            self.part = total.reshape(total.shape[: self.lead] + total.shape[-2:])

    def finish(self):
        self.land()
        while self.bit < self.bits:
            self.launch()
            self.land()
        return self.part


def place_kernel(moves, gathered_ref, *refs):
    outs, (held, in_sems, out_sems) = refs[:-3], refs[-3:]
    reads = [
        pltpu.make_async_copy(gathered_ref.at[i], held.at[i], in_sems.at[i]) for i in range(held.shape[0])
    ]
    for read in reads:
        read.start()
    writes = []
    for i, read in enumerate(reads):
        read.wait()
        for start, count, out, target in moves[i]:
            writes.append(
                pltpu.make_async_copy(
                    held.at[i, pl.ds(start, count)], outs[out].at[target], out_sems.at[len(writes)]
                )
            )
            writes[-1].start()
    for write in writes:
        write.wait()


def place(gathered, width, units):
    members, total, half = gathered.shape
    parts = members // 2
    rows = 2 * units // members
    count = width // members
    proj = shaped((3, width, half), f32)
    outs = [shaped((units, width), f32), shaped((width, units), f32), proj, proj, shaped((2, half, width), f32)]
    if count % 8 == 0 and width % rows == 0:
        moves = []
        for i in range(members):
            q, c = i // 2, i % 2
            moves.append([])
            for j in range(2):
                row = i * rows
                if row < units:
                    target = (0, (pl.ds(row, rows), pl.ds(j * half, half)))
                else:
                    block, row = divmod(row - units, width)
                    target = (1, (pl.ds(row, rows), pl.ds(block * width + j * half, half)))
                moves[i].append((j * rows, rows) + target)
            here = pl.ds(c * (width // 2) + q * count, count)
            for branch in range(2):
                start = 2 * rows + branch * 4 * count
                for a in range(3):
                    moves[i].append((start + a * count, count, 2 + branch, (a, here)))
                target = (1 - branch, pl.ds(q * count, count), pl.ds(c * half, half))
                moves[i].append((start + 3 * count, count, 4, target))
        anywhere = pl.BlockSpec(memory_space=pl.ANY)
        return pl.pallas_call(
            partial(place_kernel, moves),
            in_specs=[anywhere],
            out_specs=[anywhere] * len(outs),
            out_shape=outs,
            scratch_shapes=[
                pltpu.VMEM(gathered.shape, f32),
                pltpu.SemaphoreType.DMA((members,)),
                pltpu.SemaphoreType.DMA((sum(len(m) for m in moves),)),
            ],
            compiler_params=pltpu.CompilerParams(vmem_limit_bytes=VMEM_LIMIT),
            cost_estimate=pl.CostEstimate(flops=0, bytes_accessed=8 * gathered.size, transcendentals=0),
            name="place",
        )(gathered)
    stacked = gathered[:, : 2 * rows].reshape(members, 2, rows, half).swapaxes(1, 2).reshape(-1, width)
    fc1 = from_column_blocks(stacked[units:], units // width)
    split = gathered[:, 2 * rows :].reshape(parts, 2, 2, 4, count, half)
    projections = split[:, :, :, :3].transpose(2, 3, 1, 0, 4, 5).reshape(2, 3, width, half)
    outputs = split[:, :, ::-1, 3].transpose(2, 0, 3, 1, 4).reshape(2, half, width)
    return stacked[:units], fc1, projections[0], projections[1], outputs


def from_column_blocks(value, blocks):
    rows = value.shape[0] // blocks
    return jnp.concatenate([value[i * rows : (i + 1) * rows] for i in range(blocks)], axis=1)


def per_device(
    hidden,
    encoder,
    text_len,
    audio_len,
    corpus_weight,
    cotangent,
    norm_gain,
    norm_bias,
    self_proj,
    self_bias,
    cross_proj,
    cross_bias,
    out_proj,
    out_bias,
    fc1_weight,
    fc1_bias,
    fc2_weight,
    fc2_bias,
):
    sequences, frames, width = encoder.shape
    members = lax.axis_size("dp")
    me = lax.axis_index("dp")
    half = self_proj.shape[2]
    padded = -(-frames // FRAME_BLOCK) * FRAME_BLOCK
    core = (me & 1).astype(jnp.int32).reshape(1)

    cross_rows = jnp.concatenate(
        [cross_proj.reshape(-1, half), out_proj[1][:, :half], out_proj[1][:, half:]], axis=0
    )
    count = cross_rows.shape[0] // members
    part = lax.dynamic_slice_in_dim(cross_rows, me * count, count, 0).astype(f32)
    part = swap(jnp.concatenate([part, cross_bias], axis=0))

    normed_self, q_self, k_self, v_self, weights_self, inverse_self, heads_self, partial_self = self_forward(
        text_len, hidden, norm_gain, norm_bias, self_proj, self_bias, out_proj
    )
    part, partial_self = tie(part, partial_self)
    other_bias = part[count:]
    gathered = lax.all_gather(part[:count], "dp", axis=0, tiled=True)
    received = swap(partial_self)

    frames_in = jnp.pad(encoder.reshape(frames, width), ((0, padded - frames), (0, 0)))
    k_own = dot(frames_in, cross_proj[1], 1, 0).astype(bf16)
    v_own = (dot(frames_in, cross_proj[2], 1, 0) + cross_bias[1]).astype(bf16)
    received, k_own, v_own = tie(received, k_own, v_own)
    first, normed_cross, q_own, weights_own, inverse_own, heads_own, term_own = cross_own(
        audio_len, hidden, partial_self, received, out_bias, norm_gain, norm_bias,
        cross_proj, cross_bias, k_own, v_own, out_proj,
    )
    gathered, normed_cross = tie(gathered, normed_cross)
    (
        q_other, k_other, v_other, weights_other, inverse_other, heads_other, term_other,
        wq_other, wk_other, wv_other, wo_other,
    ) = cross_other(audio_len, normed_cross, frames_in, gathered, other_bias)

    second, partial_normed, mlp_grads, partial_mlp, fc1_bias_grad, fc2_bias_grad = feed_forward(
        text_len, corpus_weight, first, term_own, term_other, out_bias, norm_gain, norm_bias, cotangent,
        fc1_weight, fc1_bias.reshape(1, -1), fc2_weight,
    )
    received = swap(partial_normed)
    mlp_part = lax.psum_scatter(mlp_grads, "dp", scatter_dimension=0, tiled=True)

    (
        grad_second, second_low, gain_mlp, shift_mlp, bias_cross, dq_own, dk_own, dv_own, back_own,
        dq_cross_sum, dv_cross_sum, cross_theirs, cross_mine,
    ) = cross_own_back(
        text_len, corpus_weight, core, cotangent, second, partial_normed, received, norm_gain,
        out_proj, cross_proj, q_own, k_own, v_own, weights_own, inverse_own, heads_own, normed_cross, frames_in,
    )
    cross_share = Scatter(cross_theirs, cross_mine)
    cross_share.launch()
    cross_share.land()
    second_low, cross_share.theirs = tie(second_low, cross_share.theirs)
    cross_share.launch()

    (
        dk_other, dv_other, grad_first, gain_cross, shift_cross, bias_self, partial_normed,
        self_theirs, self_mine, gain_self, shift_self, dq_self_sum, dv_self_sum, *_,
    ) = other_back(
        core, second_low, wo_other, wq_other, q_other, k_other, v_other, weights_other, inverse_other, heads_other,
        back_own, first, grad_second, norm_gain, out_proj, self_proj, q_self, k_self, v_self, weights_self,
        inverse_self, heads_self, hidden, normed_self,
    )
    self_share = Scatter(self_theirs, self_mine)
    self_share.launch()
    norm_self = jnp.concatenate([gain_self, shift_self], axis=0)
    norm_received = swap(norm_self)
    norm_self, partial_normed = tie(norm_self, partial_normed)
    received = swap(partial_normed)
    self_share.land()
    cross_share.received, self_share.theirs = tie(cross_share.received, self_share.theirs)
    self_share.launch()
    cross_share.land()
    cross_share.launch()
    dk_own, cross_share.theirs = tie(dk_own, cross_share.theirs)
    grad_encoder = encoder_grad(
        dk_own, dv_own, dk_other, dv_other, cross_proj, wk_other, wv_other, frames
    ).reshape(encoder.shape)
    cross_share.received, grad_encoder = tie(cross_share.received, grad_encoder)
    cross_share.land()
    cross_share.launch()
    partial_mlp, cross_share.theirs, received = tie(partial_mlp, cross_share.theirs, received)
    received_mlp = swap(partial_mlp)

    small = (
        norm_self + norm_received,
        gain_cross,
        gain_mlp,
        shift_cross,
        shift_mlp,
        dq_self_sum,
        dv_self_sum[0:1],
        dq_cross_sum,
        dv_cross_sum[0:1],
        bias_self,
        bias_cross,
        fc1_bias_grad,
        fc2_bias_grad,
    )
    flat = jnp.concatenate([item.reshape(-1, half) for item in small], axis=0)

    unit_self, root_self = norm_unit(hidden.astype(f32))
    grad_hidden = (
        grad_first + norm_backward(partial_normed + received, unit_self, root_self, norm_gain[0])
    ).astype(bf16)
    grad_hidden, flat, self_share.received = tie(grad_hidden, flat, self_share.received)
    self_share.land()
    self_share.launch()
    cross_part = cross_share.finish()
    self_part = self_share.finish()
    rows = mlp_part.shape[0]
    every = jnp.concatenate(
        [mlp_part[:, :half], mlp_part[:, half:], cross_part.reshape(-1, half), self_part.reshape(-1, half)], axis=0
    )
    flat, every = tie(flat, every)
    every = lax.all_gather(every, "dp", axis=0, tiled=False)
    for bit in range(members.bit_length() - 1):
        flat = flat + lax.ppermute(flat, "dp", [(i, i ^ (1 << bit)) for i in range(members)])
    result = (second + (partial_mlp + received_mlp) + fc2_bias).astype(bf16)
    fc2_weight_grad, fc1_weight_grad, cross_proj_grad, self_proj_grad, out_proj_grad = place(
        every, width, fc2_weight.shape[0]
    )
    small_out = []
    offset = 0
    for item in small:
        count = item.size // half
        small_out.append(flat[offset : offset + count].reshape(item.shape))
        offset += count
    (
        norm_self, gain_cross, gain_mlp, shift_cross, shift_mlp, dq_self_sum, dv_self_sum, dq_cross_sum,
        dv_cross_sum, bias_self, bias_cross, fc1_bias_grad, fc2_bias_grad,
    ) = small_out
    return (
        result,
        grad_hidden,
        grad_encoder,
        jnp.concatenate([norm_self[0:1], gain_cross, gain_mlp], axis=0),
        jnp.concatenate([norm_self[1:2], shift_cross, shift_mlp], axis=0),
        self_proj_grad,
        jnp.concatenate([dq_self_sum, dv_self_sum], axis=0),
        cross_proj_grad,
        jnp.concatenate([dq_cross_sum, dv_cross_sum], axis=0),
        out_proj_grad,
        jnp.concatenate([bias_self, bias_cross], axis=0),
        fc1_weight_grad,
        fc1_bias_grad.reshape(-1),
        fc2_weight_grad,
        fc2_bias_grad.reshape(-1),
    )


def solution(mesh):
    placed = (
        P("dp", None),
        P("dp", None, None),
        P("dp"),
        P("dp"),
        P("dp"),
        P("dp", None),
        P(),
        P(),
        P(None, None, "tensor"),
        P(None, "tensor"),
        P(None, None, "tensor"),
        P(None, "tensor"),
        P(None, "tensor", None),
        P(),
        P(None, "tensor"),
        P("tensor"),
        P("tensor", None),
        P(),
    )
    return jax.shard_map(
        per_device,
        mesh=mesh,
        in_specs=placed,
        out_specs=(
            P("dp", None),
            P("dp", None),
            P("dp", None, None),
            P(),
            P(),
            P(None, None, "tensor"),
            P(None, "tensor"),
            P(None, None, "tensor"),
            P(None, "tensor"),
            P(None, "tensor", None),
            P(),
            P(None, "tensor"),
            P("tensor"),
            P("tensor", None),
            P(),
        ),
        check_vma=False,
    )
```

time: 630 us -> 429 us (0.68)
  waiting for transfers between devices: 366 us -> 220 us
  Pallas kernels: 55.4 us -> 128 us
  local copies, waits for them, and re-layouts: 78.6 us -> 22.5 us
  matrix products: 54.3 us -> 4.87 us
  other arithmetic: 38.5 us -> 16.4 us
    ppermute x12, waiting for transfers between devices: 236 us -> 80.5 us  [the longest x8 70.7 us: launch(): lax.ppermute(self.theirs, 'dp', [(i, i ^ other) for i in range(self.membe...]
    pallas_call x6 -> x8, Pallas kernels: 55.4 us -> 128 us  [the longest x6 103 us: call(): pl.pallas_call(body, in_specs=[pl.BlockSpec(memory_space=pltpu.SMEM)] * l...]
    dot_general x30 -> x2, matrix products: 54.3 us -> 4.87 us  [dot(): lax.dot_general(a, b, (((ca,), (cb,)), ((), ())), preferred_element_type=...]
    all_gather x4 -> x2, waiting for transfers between devices: 36.2 us -> 66.8 us  [the longest x1 61.1 us: per_device(): every = lax.all_gather(every, 'dp', axis=0, tiled=False)]
    unnamed x133 -> x70, local copies, waits for them, and re-layouts: 37.6 us -> 7.4 us
    slice x29 -> x10, local copies, waits for them, and re-layouts: 30.1 us -> 5.25 us  [the longest x1 1.09 us: per_device(): mlp_part[:, :half]]
    ppermute x6, waiting for transfers between devices: 94.2 us -> 72.4 us  [swap(): return lax.ppermute(value, 'tensor', [(0, 1), (1, 0)])]
    reduce_sum x12 -> x2, other arithmetic: 10.3 us -> 0.53 us  [the longest x1 0.36 us: norm_unit(): jnp.mean(centered * centered, axis=-1, keepdims=True) + epsilon]
  transfers between devices with their start and end apart: 22 -> 21, of which waited for: 17 -> 14; matrix products, arithmetic and copies ran while one was open for 16% -> 8% of each run, Pallas kernels for 1% -> 19%
where the time goes in v2:
time: 429 us; the launch traced here: 424 us
  waiting for transfers between devices  220 us (51%)
  Pallas kernels  128 us (30%)
  local copies, waits for them, and re-layouts  22.5 us (5%)
  between operations  16.6 us (4%)
  other arithmetic  16.4 us (4%)
  starting transfers between devices  16.3 us (4%)
  matrix products  4.87 us (1%)
    pallas_call x6, Pallas kernels, call(): pl.pallas_call(body, in_specs=[pl.BlockSpec(memory_space=pltpu.SMEM)] * l...  103 us
    ppermute x6, waiting for transfers between devices, swap(): return lax.ppermute(value, 'tensor', [(0, 1), (1, 0)])  72.4 us
    ppermute x8, waiting for transfers between devices, launch(): lax.ppermute(self.theirs, 'dp', [(i, i ^ other) for i in range(self.membe...  70.7 us
    all_gather x1, waiting for transfers between devices, per_device(): every = lax.all_gather(every, 'dp', axis=0, tiled=False)  61.1 us
    pallas_call x1, Pallas kernels, place(): pl.pallas_call(partial(place_kernel, moves), in_specs=[anywhere], out_spe...  14.5 us
    pallas_call x1, Pallas kernels, encoder_grad(): pl.pallas_call(encoder_grad_kernel, grid=(padded // FRAME_BLOCK,), in_spe...  10.6 us
    ppermute x4, waiting for transfers between devices, per_device(): lax.ppermute(flat, 'dp', [(i, i ^ 1 << bit) for i in range(members)])  9.78 us
  transfers between devices with their start and end apart: 21, of which 14 were waited for; matrix products, arithmetic and copies ran while one was open for 8% of the time, Pallas kernels for 19%

profile of v2, /device:TPU:0, one launch (start us, length us, event | category | flops | bytes accessed | tf_op | source)
XLA Modules:
  0.0 424.2 jit_solution(4462291152748042471)
XLA Ops:
  9.3 3.0 collective-permute-start
  13.0 7.5 %self_forward.1 = (bf16[448,768]{1,0:T(8,128)(2,1)}, bf16[448,384]{1,0:T(8,128)(2,1)}, bf16[448,384]{1,0:T(8,128)(2,1)}, bf16[448,384]{1,0:T(8,128)(2,1)}, bf16[...) custom-call(s32[1]{0:T(128)S(6)} %copy.41.refs_0_, ...), custom_call_target="tpu_custom_call" | custom-call | flops 30965760 | bytes 159312 | tf_op jit(solution)/shard_map/self_forward/pallas_call | solution.py:124
  24.3 3.4 pad.4.refs_3_.refs_17_
  27.7 2.5 convolution_convert_fusion.refs_9_.refs_10_
  30.2 2.4 fusion.refs_10_.refs_11_
  33.2 20.3 %collective-permute-done.1.refs_1_ = f32[448,768]{1,0:T(8,128)S(1)} collective-permute-done((f32[448,768]{1,0:T(8,128)}, f32[448,768]{1,0:T(8,128)S(1)}, u32[]{:S(2)}, u32[]{:S(2)}) %collective-permute-start.1) | collective-permute-done | bytes 1376288 | tf_op jit(solution)/shard_map/ppermute | solution.py:699
  54.6 15.0 %cross_own.1 = (f32[448,768]{1,0:T(8,128)}, bf16[448,768]{1,0:T(8,128)(2,1)}, bf16[448,384]{1,0:T(8,128)(2,1)}, bf16[6,448,1536]{2,1,0:T(8,128)(2,1)}, f32[448,3...) custom-call(s32[1]{0:T(128)S(6)} %copy.42.refs_0_, f32[448,768]{1,0:T(8,128)} %copy-done.11, ...), custom_call_target="tpu_custom_call" | custom-call | flops 57802752 | bytes 341424 | tf_op jit(solution)/shard_map/cross_own/pallas_call | solution.py:124
  69.6 5.7 %all-gather.4.cloned.1.call-done.refs_1_ = f32[3072,384]{1,0:T(8,128)} async-done(((f32[192,384]{1,0:T(8,128)}), f32[3072,384]{1,0:T(8,128)}) %all-gather.4.cloned.1.call-update) | async-done | bytes 4718608 | tf_op jit(solution)/shard_map/all_gather | solution.py:860
  75.3 15.3 %cross_other.1 = (bf16[448,384]{1,0:T(8,128)(2,1)}, bf16[1536,384]{1,0:T(8,128)(2,1)}, bf16[1536,384]{1,0:T(8,128)(2,1)}, bf16[6,448,1536]{2,1,0:T(8,128)(2,1)},...) custom-call(s32[1]{0:T(128)S(6)} %copy.42.refs_0_, ...), custom_call_target="tpu_custom_call" | custom-call | flops 86114304 | bytes 367152 | tf_op jit(solution)/shard_map/cross_other/pallas_call | solution.py:124
  90.6 18.6 %feed_forward.1 = (f32[448,768]{1,0:T(8,128)}, f32[448,768]{1,0:T(8,128)}, f32[3072,768]{1,0:T(8,128)}, f32[448,768]{1,0:T(8,128)}, f32[1,1536]{1,0:T(1,128)}, /*index=5*/f32[1,768]{1,0:T(1,128)}) custom-call(s32[1]{0:T(128)S(6)} %copy.41.refs_0_, f32[1]{0:T(128)S(6)} %copy.43.refs_1_, f32[448,768]{1,0:T(8,128)} %get-tuple-element.105.refs_2_, ...), custom_call_target="tpu_custom_call" | custom-call | flops 99090432 | bytes 361584 | tf_op jit(solution)/shard_map/feed_forward/pallas_call | solution.py:124
  112.1 30.9 %collective-permute-done.2.refs_3_ = f32[448,768]{1,0:T(8,128)S(1)} collective-permute-done((f32[448,768]{1,0:T(8,128)S(1)}, f32[448,768]{1,0:T(8,128)S(1)}, u32[]{:S(2)}, u32[]{:S(2)}) %collective-permute-start.2) | collective-permute-done | bytes 1376288 | tf_op jit(solution)/shard_map/ppermute | solution.py:699
  144.0 21.7 %cross_own_back.1 = (f32[448,768]{1,0:T(8,128)}, bf16[448,768]{1,0:T(8,128)(2,1)}, f32[1,768]{1,0:T(1,128)}, f32[1,768]{1,0:T(1,128)}, f32[1,768]{1,0:T(1,128)},...) custom-call(s32[1]{0:T(128)S(6)} %copy.41.refs_0_, ...), custom_call_target="tpu_custom_call" | custom-call | flops 143917056 | bytes 526584 | tf_op jit(solution)/shard_map/cross_own_back/pallas_call | solution.py:124
  165.8 4.7 %collective-permute-done.3 = f32[4,384,384]{2,1,0:T(8,128)S(1)} collective-permute-done((f32[4,384,384]{2,1,0:T(8,128)}, f32[4,384,384]{2,1,0:T(8,128)S(1)}, u32[]{:S(2)}, u32[]{:S(2)}) %collective-permute-start.3) | collective-permute-done | bytes 2359328 | tf_op jit(solution)/shard_map/ppermute | solution.py:717
  170.5 1.9 add.121
  174.2 24.5 %other_back.1 = (bf16[384,1536]{1,0:T(8,128)(2,1)}, bf16[384,1536]{1,0:T(8,128)(2,1)}, f32[448,768]{1,0:T(8,128)}, f32[1,768]{1,0:T(1,128)}, f32[1,768]{1,0:T(1,...) custom-call(s32[1]{0:T(128)} %bitcast.5.refs_2_.refs_0_, ...), custom_call_target="tpu_custom_call" | custom-call | flops 169279488 | bytes 599640 | tf_op jit(solution)/shard_map/other_back/pallas_call | solution.py:124
  200.0 1.5 collective-permute-start.7
  201.5 2.0 collective-permute-done.5
  204.9 2.6 add.124
  208.7 22.1 %collective-permute-done.4 = f32[4,2,2,1,48,384]{5,4,3,2,1,0:T(8,128)} collective-permute-done((f32[4,2,2,1,48,384]{5,4,3,2,1,0:T(8,128)}, f32[4,2,2,1,48,384]{5,4,3,2,1,0:T(8,128)}, u32[]{:S(2)}, u32[]{:S(2)}) %collective-permute-start.4) | collective-permute-done | bytes 1179680 | tf_op jit(solution)/shard_map/ppermute | solution.py:717
  234.1 1.5 collective-permute-start.6
  235.6 1.5 collective-permute-start.9
  240.3 10.6 %encoder_grad.1 = f32[1500,1,768]{2,1,0:T(1,128)} custom-call(bf16[384,1536]{1,0:T(8,128)(2,1)} %get-tuple-element.145.dk0_ref, bf16[384,1536]{1,0:T(8,128)(2,1)} %get-tuple-element.146.dv0_ref, bf16[384,1536]{1,0:T(8,128)(2,1)} %get-tuple-element.147.dk1_ref, bf16[384,1536]{1,0:T(8,128)(2,1)} %get-tuple-element.148.dv1_ref, bf16[3,768,384]{2,1,0:T(8,128)(2,1)} %proj_ref.1, ...), custom_call_target="tpu_custom_call" | custom-call | flops 3623878656 | bytes 6912000 | tf_op jit(solution)/shard_map/encoder_grad/pallas_call | solution.py:684
  252.2 2.5 fusion.20
  256.0 11.2 %collective-permute-done.10 = f32[4,2,2,1,48,384]{5,4,3,2,1,0:T(8,128)S(1)} collective-permute-done((f32[4,2,2,1,48,384]{5,4,3,2,1,0:T(8,128)}, f32[4,2,2,1,48,384]{5,4,3,2,1,0:T(8,128)S(1)}, u32[]{:S(2)}, u32[]{:S(2)}) %collective-permute-start.10) | collective-permute-done | bytes 1179680 | tf_op jit(solution)/shard_map/ppermute | solution.py:717
  268.0 2.4 collective-permute-start.11
  270.4 17.0 %collective-permute-done.12 = f32[4,2,1,1,48,384]{5,4,3,2,1,0:T(8,128)S(1)} collective-permute-done((f32[4,2,1,1,48,384]{5,4,3,2,1,0:T(8,128)S(1)}, f32[4,2,1,1,48,384]{5,4,3,2,1,0:T(8,128)S(1)}, u32[]{:S(2)}, u32[]{:S(2)}) %collective-permute-start.12) | collective-permute-done | bytes 589856 | tf_op jit(solution)/shard_map/ppermute | solution.py:717
  288.1 13.8 %collective-permute-done.13 = f32[4,1,1,1,48,384]{5,4,3,2,1,0:T(8,128)S(1)} collective-permute-done((f32[4,1,1,1,48,384]{5,4,3,2,1,0:T(8,128)S(1)}, f32[4,1,1,1,48,384]{5,4,3,2,1,0:T(8,128)S(1)}, u32[]{:S(2)}, u32[]{:S(2)}) %collective-permute-start.13) | collective-permute-done | bytes 294944 | tf_op jit(solution)/shard_map/ppermute | solution.py:717
  306.7 3.5 collective-permute-done.15
  310.3 5.1 %collective-permute-done.16 = f32[26,384]{1,0:T(8,128)S(1)} collective-permute-done((f32[26,384]{1,0:T(8,128)S(1)}, f32[26,384]{1,0:T(8,128)S(1)}, u32[]{:S(2)}, u32[]{:S(2)}) %collective-permute-start.16) | collective-permute-done | bytes 39968 | tf_op jit(solution)/shard_map/ppermute | solution.py:959
  315.7 21.2 %collective-permute-done.8 = f32[448,768]{1,0:T(8,128)S(1)} collective-permute-done((f32[448,768]{1,0:T(8,128)S(1)}, f32[448,768]{1,0:T(8,128)S(1)}, u32[]{:S(2)}, u32[]{:S(2)}) %collective-permute-start.8) | collective-permute-done | bytes 1376288 | tf_op jit(solution)/shard_map/ppermute | solution.py:699
  341.9 61.1 %all-gather.6.cloned.1.call-done = f32[12288,384]{1,0:T(8,128)} async-done(((f32[768,384]{1,0:T(8,128)}), f32[12288,384]{1,0:T(8,128)}) %all-gather.6.cloned.1.call-update) | async-done | bytes 18874384 | tf_op jit(solution)/shard_map/all_gather | solution.py:957
  403.0 14.5 %place.1 = (f32[1536,768]{1,0:T(8,128)}, f32[768,1536]{1,0:T(8,128)}, f32[3,768,384]{2,1,0:T(8,128)}, f32[3,768,384]{2,1,0:T(8,128)}, f32[2,384,768]{2,1,0:T(8,128)}) custom-call(f32[16,768,384]{2,1,0:T(8,128)} %bitcast.49), custom_call_target="tpu_custom_call" | custom-call | bytes 37748736 | tf_op jit(solution)/shard_map/place/pallas_call | solution.py:794
  (160 shorter events, 36.2 us)
Async XLA Ops:
  7.2 68.1 %all-gather.4.cloned.1.call-start = ((), (), s32[]{:S(2)}) async-start(), calls=%async_computation.1 | async-start | bytes 5013504 | tf_op jit(solution)/shard_map/all_gather | solution.py:860
  9.3 11.2 %collective-permute-start = (f32[194,384]{1,0:T(8,128)S(1)}, f32[194,384]{1,0:T(8,128)S(1)}, u32[]{:S(2)}, u32[]{:S(2)}) collective-permute-start(f32[194,384]{1,0:T(8,128)S(1)} %pad_maximum_fusion.1), channel_id=1, source_target_pairs={{0,1},{1,0},{2,3},{3,2},{4,5},{5,4},{6,7},{7,6},{8,9},{9,8},{10,11... | collective-permute-start | bytes 893960 | tf_op jit(solution)/shard_map/ppermute | solution.py:699
  21.4 280.5 %reduce-scatter.2.cloned.1.call-start = ((), (), s32[]{:S(2)}) async-start(), calls=%async_computation.2 | async-start | bytes 10027008 | tf_op jit(solution)/shard_map/reduce_scatter | solution.py:882
  21.6 31.9 %collective-permute-start.1 = (f32[448,768]{1,0:T(8,128)}, f32[448,768]{1,0:T(8,128)S(1)}, u32[]{:S(2)}, u32[]{:S(2)}) collective-permute-start(f32[448,768]{1,0:T(8,128)} %get-tuple-element.101.refs_2_), channel_id=1, source_target_pairs={{0,1},{1,0},{2,3},{3,2},{4,5},{5,4},{6,7},{7,6},{8,9},{9,8},{10,11... | collective-permute-start | bytes 4128776 | tf_op jit(solution)/shard_map/ppermute | solution.py:699
  109.3 293.7 %all-gather.6.cloned.1.call-start = ((), (), s32[]{:S(2)}) async-start(), calls=%async_computation.3 | async-start | bytes 20054016 | tf_op jit(solution)/shard_map/all_gather | solution.py:957
  110.6 32.3 %collective-permute-start.2 = (f32[448,768]{1,0:T(8,128)S(1)}, f32[448,768]{1,0:T(8,128)S(1)}, u32[]{:S(2)}, u32[]{:S(2)}) collective-permute-start(f32[448,768]{1,0:T(8,128)S(1)} %copy-done.14), channel_id=1, source_target_pairs={{0,1},{1,0},{2,3},{3,2},{4,5},{5,4},{6,7},{7,6},{8,9},{9,8},{10,11... | collective-permute-start | bytes 4128776 | tf_op jit(solution)/shard_map/ppermute | solution.py:699
  165.7 4.8 %collective-permute-start.3 = (f32[4,384,384]{2,1,0:T(8,128)}, f32[4,384,384]{2,1,0:T(8,128)S(1)}, u32[]{:S(2)}, u32[]{:S(2)}) collective-permute-start(f32[4,384,384]{2,1,0:T(8,128)} %get-tuple-element.120), channel_id=1, source_target_pairs={{0,2},{2,0},{4,6},{6,4},{8,10},{10,8},{12,14},{14,12},{16,18},{18,... | collective-permute-start | bytes 7077896 | tf_op jit(solution)/shard_map/ppermute | solution.py:717
  174.2 25.2 %copy-start = (bf16[448,768]{1,0:T(8,128)(2,1)S(1)}, bf16[448,768]{1,0:T(8,128)(2,1)}, u32[]{:S(2)}) copy-start(bf16[448,768]{1,0:T(8,128)(2,1)} %refs_22_.1) | copy-start | bytes 2064388
  198.7 4.8 %collective-permute-start.5 = (f32[4,384,384]{2,1,0:T(8,128)}, f32[4,384,384]{2,1,0:T(8,128)S(1)}, u32[]{:S(2)}, u32[]{:S(2)}) collective-permute-start(f32[4,384,384]{2,1,0:T(8,128)} %get-tuple-element.142), channel_id=1, source_target_pairs={{0,2},{2,0},{4,6},{6,4},{8,10},{10,8},{12,14},{14,12},{16,18},{18,... | collective-permute-start | bytes 7077896 | tf_op jit(solution)/shard_map/ppermute | solution.py:717
  198.9 31.8 %collective-permute-start.4 = (f32[4,2,2,1,48,384]{5,4,3,2,1,0:T(8,128)}, f32[4,2,2,1,48,384]{5,4,3,2,1,0:T(8,128)}, u32[]{:S(2)}, u32[]{:S(2)}) collective-permute-start(f32[4,2,2,1,48,384]{5,4,3,2,1,0:T(8,128)} %constant_dynamic-slice_fusion.5), channel_id=1, source_target_pairs={{0,4},{2,6},{4,0},{6,2},{8,12},{10,14},{12,8},{14,10},{16,20},{18,... | collective-permute-start | bytes 3538952 | tf_op jit(solution)/shard_map/ppermute | solution.py:717
  200.0 52.2 %collective-permute-start.7 = (f32[448,768]{1,0:T(8,128)}, f32[448,768]{1,0:T(8,128)}, u32[]{:S(2)}, u32[]{:S(2)}) collective-permute-start(f32[448,768]{1,0:T(8,128)} %get-tuple-element.155), channel_id=1, source_target_pairs={{0,1},{1,0},{2,3},{3,2},{4,5},{5,4},{6,7},{7,6},{8,9},{9,8},{10,11... | collective-permute-start | bytes 4128776 | tf_op jit(solution)/shard_map/ppermute | solution.py:699
  208.6 29.1 %copy-start.20 = (f32[1,768]{1,0:T(1,128)S(1)}, f32[1,768]{1,0:T(1,128)}, u32[]{:S(2)}) copy-start(f32[1,768]{1,0:T(1,128)} %get-tuple-element.171) | copy-start | bytes 9220
  208.6 29.2 %copy-start.18 = (f32[1,1536]{1,0:T(1,128)S(1)}, f32[1,1536]{1,0:T(1,128)}, u32[]{:S(2)}) copy-start(f32[1,1536]{1,0:T(1,128)} %get-tuple-element.170) | copy-start | bytes 18436
  208.6 29.9 %copy-start.23 = (f32[1,768]{1,0:T(1,128)S(1)}, f32[1,768]{1,0:T(1,128)}, u32[]{:S(2)}) copy-start(f32[1,768]{1,0:T(1,128)} %get-tuple-element.161) | copy-start | bytes 9220
  208.6 30.0 %copy-start.22 = (f32[1,768]{1,0:T(1,128)S(1)}, f32[1,768]{1,0:T(1,128)}, u32[]{:S(2)}) copy-start(f32[1,768]{1,0:T(1,128)} %get-tuple-element.163) | copy-start | bytes 9220
  208.7 30.0 %copy-start.21 = (f32[1,768]{1,0:T(1,128)S(1)}, f32[1,768]{1,0:T(1,128)}, u32[]{:S(2)}) copy-start(f32[1,768]{1,0:T(1,128)} %get-tuple-element.169) | copy-start | bytes 9220
  208.7 30.8 %copy-start.26 = (f32[1,768]{1,0:T(1,128)S(1)}, f32[1,768]{1,0:T(1,128)}, u32[]{:S(2)}) copy-start(f32[1,768]{1,0:T(1,128)} %get-tuple-element.160) | copy-start | bytes 9220
  208.7 30.8 %copy-start.25 = (f32[1,768]{1,0:T(1,128)S(1)}, f32[1,768]{1,0:T(1,128)}, u32[]{:S(2)}) copy-start(f32[1,768]{1,0:T(1,128)} %get-tuple-element.162) | copy-start | bytes 9220
  208.7 30.8 %copy-start.24 = (f32[1,768]{1,0:T(1,128)S(1)}, f32[1,768]{1,0:T(1,128)}, u32[]{:S(2)}) copy-start(f32[1,768]{1,0:T(1,128)} %get-tuple-element.168) | copy-start | bytes 9220
  234.1 16.9 %collective-permute-start.6 = (f32[4,2,1,1,48,384]{5,4,3,2,1,0:T(8,128)}, f32[4,2,1,1,48,384]{5,4,3,2,1,0:T(8,128)}, u32[]{:S(2)}, u32[]{:S(2)}) collective-permute-start(f32[4,2,1,1,48,384]{5,4,3,2,1,0:T(8,128)} %constant_dynamic-slice_fusion.3), channel_id=1, source_target_pairs={{0,8},{2,10},{4,12},{6,14},{8,0},{10,2},{12,4},{14,6},{16,24},{18,... | collective-permute-start | bytes 1769480 | tf_op jit(solution)/shard_map/ppermute | solution.py:717
  235.6 4.0 collective-permute-start.9
  239.7 27.5 %collective-permute-start.10 = (f32[4,2,2,1,48,384]{5,4,3,2,1,0:T(8,128)}, f32[4,2,2,1,48,384]{5,4,3,2,1,0:T(8,128)S(1)}, u32[]{:S(2)}, u32[]{:S(2)}) collective-permute-start(f32[4,2,2,1,48,384]{5,4,3,2,1,0:T(8,128)} %constant_dynamic-slice_fusion.4), channel_id=1, source_target_pairs={{0,4},{2,6},{4,0},{6,2},{8,12},{10,14},{12,8},{14,10},{16,20},{18,... | collective-permute-start | bytes 3538952 | tf_op jit(solution)/shard_map/ppermute | solution.py:717
  267.4 20.0 %collective-permute-start.12 = (f32[4,2,1,1,48,384]{5,4,3,2,1,0:T(8,128)S(1)}, f32[4,2,1,1,48,384]{5,4,3,2,1,0:T(8,128)S(1)}, u32[]{:S(2)}, u32[]{:S(2)}) collective-permute-start(f32[4,2,1,1,48,384]{5,4,3,2,1,0:T(8,128)S(1)} %constant_dynamic-slice_fusion.1), channel_id=1, source_target_pairs={{0,8},{2,10},{4,12},{6,14},{8,0},{10,2},{12,4},{14,6},{16,24},{18,... | collective-permute-start | bytes 1769480 | tf_op jit(solution)/shard_map/ppermute | solution.py:717
  268.0 20.1 %collective-permute-start.11 = (f32[4,1,1,1,48,384]{5,4,3,2,1,0:T(8,128)S(1)}, f32[4,1,1,1,48,384]{5,4,3,2,1,0:T(8,128)S(1)}, u32[]{:S(2)}, u32[]{:S(2)}) collective-permute-start(f32[4,1,1,1,48,384]{5,4,3,2,1,0:T(8,128)S(1)} %constant_dynamic-slice_fusion.2), channel_id=1, source_target_pairs={{0,16},{2,18},{4,20},{6,22},{8,24},{10,26},{12,28},{14,30},{16,0},... | collective-permute-start | bytes 884744 | tf_op jit(solution)/shard_map/ppermute | solution.py:717
  287.5 14.3 %collective-permute-start.13 = (f32[4,1,1,1,48,384]{5,4,3,2,1,0:T(8,128)S(1)}, f32[4,1,1,1,48,384]{5,4,3,2,1,0:T(8,128)S(1)}, u32[]{:S(2)}, u32[]{:S(2)}) collective-permute-start(f32[4,1,1,1,48,384]{5,4,3,2,1,0:T(8,128)S(1)} %constant_dynamic-slice_fusion), channel_id=1, source_target_pairs={{0,16},{2,18},{4,20},{6,22},{8,24},{10,26},{12,28},{14,30},{16,0},... | collective-permute-start | bytes 884744 | tf_op jit(solution)/shard_map/ppermute | solution.py:717
  304.1 32.8 %copy-start.4 = (f32[448,768]{1,0:T(8,128)S(1)}, f32[448,768]{1,0:T(8,128)}, u32[]{:S(2)}) copy-start(f32[448,768]{1,0:T(8,128)} %get-tuple-element.112.refs_5_) | copy-start | bytes 4128772
  304.1 32.8 %copy-start.19 = (f32[768]{0:T(1024)S(1)}, f32[768]{0:T(1024)}, u32[]{:S(2)}) copy-start(f32[768]{0:T(1024)} %param.35) | copy-start | bytes 9220
  304.8 32.1 %collective-permute-start.8 = (f32[448,768]{1,0:T(8,128)S(1)}, f32[448,768]{1,0:T(8,128)S(1)}, u32[]{:S(2)}, u32[]{:S(2)}) collective-permute-start(f32[448,768]{1,0:T(8,128)S(1)} %copy-done.12), channel_id=1, source_target_pairs={{0,1},{1,0},{2,3},{3,2},{4,5},{5,4},{6,7},{7,6},{8,9},{9,8},{10,11... | collective-permute-start | bytes 4128776 | tf_op jit(solution)/shard_map/ppermute | solution.py:699
  304.8 1.2 collective-permute-start.14
  306.0 4.2 collective-permute-start.15
  310.2 5.2 %collective-permute-start.16 = (f32[26,384]{1,0:T(8,128)S(1)}, f32[26,384]{1,0:T(8,128)S(1)}, u32[]{:S(2)}, u32[]{:S(2)}) collective-permute-start(f32[26,384]{1,0:T(8,128)S(1)} %add.145), channel_id=1, source_target_pairs={{0,8},{2,10},{4,12},{6,14},{8,0},{10,2},{12,4},{14,6},{16,24},{18,... | collective-permute-start | bytes 119816 | tf_op jit(solution)/shard_map/ppermute | solution.py:959
  315.4 22.8 %collective-permute-start.17 = (f32[26,384]{1,0:T(8,128)S(1)}, f32[26,384]{1,0:T(8,128)S(1)}, u32[]{:S(2)}, u32[]{:S(2)}) collective-permute-start(f32[26,384]{1,0:T(8,128)S(1)} %add.146), channel_id=1, source_target_pairs={{0,16},{2,18},{4,20},{6,22},{8,24},{10,26},{12,28},{14,30},{16,0},... | collective-permute-start | bytes 119816 | tf_op jit(solution)/shard_map/ppermute | solution.py:959
  (20 other events, 100.9 us)
Sparse Core Ops, SparseCore 0:
  21.5 53.7 all-gather.3
  109.4 111.7 reduce-scatter.1
  304.3 98.6 all-gather.5
